TPU v7x, 256 devices: a whole 4x4x8 slice. The times are simulated.
256 devices in a mesh: frame: 16 (over x_lo, y, core), tile: 16 (over z, x_hi).
Axes of the slice: x: 4 (x_hi: 2, x_lo: 2; x = x_hi * 2 + x_lo), y: 4, z: 8, core: 2. Of those that a mesh axis runs over, the one named last changes fastest.
Arguments:
- features: bfloat16 [16, 32, 16384], P('frame', None, 'tile'), may hold values from -6 to 6
- views: int32 [16, 4], replicated, may hold values from 0 to 15, as said below
- offsets: int32 [16, 4, 32, 128], P('frame', None, None, 'tile'), may hold values from -2 to 2
- kernels: bfloat16 [32, 128, 128], replicated, may hold values from -0.5 to 0.5
- reg_weight: bfloat16 [3, 8, 32], replicated, may hold values from -0.625 to 0.625
- head_weight: float32 [8], replicated, may hold values from -2 to 2
- depth_cot: float32 [16, 16384], P('frame', 'tile'), may hold values from -120 to 120
Outputs:
- depth: float32 [16, 16384], P('frame', 'tile')
- feature_grad: float32 [16, 32, 16384], P('frame', None, 'tile')
Inputs may be any that keep to these rules, and one draw needn't show every extreme that they name: `views`: row f lists 4 different frames, none of them f.
All inputs are finite; a program needn't handle non-finite values.
Results may differ from a plain program's by a relative error of at most 0.017.
The roundings to bfloat16 on the way count: a program that leaves them out, or rounds other values in their place, can miss the bound.
Values may be sent and summed in bfloat16 or wider, within the bound.
A program may use at most 64 MiB of HBM per device.

v0:
```python
import jax
import jax.numpy as jnp
from jax import lax
from jax.sharding import PartitionSpec as P

V = 4
HB = 2


def padded_2(cells, sides, width):
    for axis, dim in sides:
        count = lax.axis_size(axis)
        ends = count - 1
        head = lax.slice_in_dim(cells, 0, width, axis=dim)
        tail = lax.slice_in_dim(cells, cells.shape[dim] - width, cells.shape[dim], axis=dim)
        cells = jnp.concatenate(
            [
                lax.ppermute(tail, axis, [(i, (i + 1) % count) for i in range(ends)]),
                cells,
                lax.ppermute(head, axis, [((i + 1) % count, i) for i in range(ends)]),
            ],
            axis=dim,
        )
    return cells


def passed_along(block, axis, distance):
    devices = range(lax.axis_size(axis))
    route = [((i - distance) % len(devices), i) for i in devices]
    return lax.ppermute(block, axis, route)


def warp_block(reference_feat, sources, block_index, kernel):
    frames, vcount, channels, padded_len = sources.shape
    blocks = sources.reshape(frames, vcount, channels, padded_len // 128, 128)
    picker = jax.vmap(jax.vmap(lambda blockset, where_at: jnp.take(blockset, where_at, axis=1)))
    picked = picker(blocks, block_index).astype(jnp.bfloat16)
    pixels = block_index.shape[2] * 128
    warped = jnp.dot(picked.reshape(-1, 128), kernel, preferred_element_type=jnp.float32)
    warped = warped.reshape(frames, vcount, channels, pixels)
    stacked = jnp.concatenate([reference_feat[:, None], warped], axis=1)
    average = jnp.sum(stacked, axis=1) / (V + 1)
    centred = stacked - average[:, None]
    return (jnp.sum(centred * centred, axis=1) / (V + 1)).astype(jnp.bfloat16)


def local_depth(reference_feat, sources, offsets, kernels, reg_weight, head_weight):
    block_count = offsets.shape[3]
    plane_count = kernels.shape[0]
    base_index = jnp.arange(block_count, dtype=jnp.int32) + HB
    plane_index = jnp.transpose(offsets, (2, 0, 1, 3)) + base_index

    def per_plane(plane_items):
        return warp_block(reference_feat, sources, plane_items[0], plane_items[1])

    volume = lax.map(jax.checkpoint(per_plane), (plane_index, kernels))
    padded = jnp.pad(volume, ((1, 1), (0, 0), (0, 0), (0, 0)))
    hidden = jnp.einsum(
        "rc,dacp->darp", reg_weight[0], padded[0:plane_count], preferred_element_type=jnp.float32
    )
    for tap_index in range(1, 3):
        hidden = hidden + jnp.einsum(
            "rc,dacp->darp",
            reg_weight[tap_index],
            padded[tap_index : tap_index + plane_count],
            preferred_element_type=jnp.float32,
        )
    scores = 4.0 * jnp.tanh(jnp.sum(hidden * head_weight[None, None, :, None], axis=2))
    weights = jnp.exp(scores)
    values = (jnp.arange(plane_count, dtype=jnp.float32) + 1.0) / plane_count
    return jnp.sum(weights * values[:, None, None], axis=0) / jnp.sum(weights, axis=0)


def per_device(features, views, offsets, kernels, reg_weight, head_weight, depth_cot):
    local_frames, channels, pixels = features.shape
    rim_width = HB * 128
    frame_pos = lax.axis_index("frame")
    frame_count = lax.axis_size("frame")
    my_views = lax.dynamic_slice_in_dim(views, frame_pos * local_frames, local_frames, 0)
    owners = my_views // local_frames
    slot_ids = my_views % local_frames
    slot_range = jnp.arange(local_frames, dtype=jnp.int32)
    padded = padded_2(features, (("tile", 2),), rim_width)
    gathered = jnp.zeros((local_frames, V, channels, padded.shape[2]), jnp.bfloat16)

    def choose(current, travelling, source_dev):
        matches = (owners == source_dev)[:, :, None] & (
            slot_ids[:, :, None] == slot_range[None, None, :]
        )
        selector = matches.astype(jnp.bfloat16)
        taken = jnp.einsum(
            "ajk,kcp->ajcp", selector, travelling, preferred_element_type=jnp.float32
        ).astype(jnp.bfloat16)
        return jnp.where(jnp.any(matches, axis=2)[:, :, None, None], taken, current)

    gathered = choose(gathered, padded, frame_pos)

    def cycle_step(step_num, carry):
        travelling, current = carry
        travelling = passed_along(travelling, "frame", 1)
        return (travelling, choose(current, travelling, (frame_pos - step_num) % frame_count))

    gathered = lax.fori_loop(1, frame_count, cycle_step, (padded, gathered))[1]
    ref_copy = features.astype(jnp.float32)
    src_copy = gathered.astype(jnp.float32)
    depth_map, pullback = jax.vjp(
        lambda ref_part, src_part: local_depth(
            ref_part, src_part, offsets, kernels, reg_weight, head_weight
        ),
        ref_copy,
        src_copy,
    )
    ref_grad, src_grad = pullback(depth_cot)

    def contribution(dest_dev):
        matches = (owners == dest_dev)[:, :, None] & (
            slot_ids[:, :, None] == slot_range[None, None, :]
        )
        return jnp.einsum(
            "ajk,ajcp->kcp", matches.astype(jnp.float32), src_grad, precision=lax.Precision.HIGHEST
        )

    returned = contribution((frame_pos - 1) % frame_count)

    def back_step(step_num, summed):
        summed = passed_along(summed.astype(jnp.bfloat16), "frame", 1).astype(summed.dtype)
        return summed + contribution((frame_pos - step_num - 1) % frame_count)

    returned = lax.fori_loop(1, frame_count, back_step, returned)
    core_grad = returned[:, :, rim_width : rim_width + pixels] + ref_grad
    rim_pair = jnp.concatenate(
        [returned[:, :, :rim_width], returned[:, :, rim_width + pixels :]], axis=2
    )
    rim_halo = padded_2(rim_pair.astype(jnp.bfloat16), (("tile", 2),), rim_width).astype(
        rim_pair.dtype
    )
    from_prev = rim_halo[:, :, :rim_width]
    from_next = rim_halo[:, :, 3 * rim_width :]
    core_grad = core_grad + jnp.pad(from_prev, ((0, 0), (0, 0), (0, pixels - rim_width)))
    core_grad = core_grad + jnp.pad(from_next, ((0, 0), (0, 0), (pixels - rim_width, 0)))
    return (depth_map, core_grad)


def solution(mesh):
    return jax.shard_map(
        per_device,
        mesh=mesh,
        in_specs=(
            P("frame", None, "tile"),
            P(),
            P("frame", None, None, "tile"),
            P(),
            P(),
            P(),
            P("frame", "tile"),
        ),
        out_specs=(P("frame", "tile"), P("frame", None, "tile")),
        check_vma=False,
    )
```

profile of v0, /device:TPU:100, one launch (start us, length us, event | category | flops | bytes accessed | tf_op | source)
XLA Modules:
  0.0 601.1 jit_solution(12528834087215389453)
XLA Ops:
  1.4 5.0 collective-permute-start.2
  6.4 2.4 collective-permute-start.3
  10.8 4.8 collective-permute-done.3
  15.8 96.6 %while.59 = (s32[]{:T(128)}, bf16[1,32,1536]{2,1,0:T(8,128)(2,1)S(1)}, bf16[1,4,32,1536]{3,2,1,0:T(8,128)(2,1)S(1)}, s32[]{:T(128)}, s32[1,4]{1,0:T(1,128)S(1)},...) while((s32[]{:T(128)}, bf16[1,32,1536]{2,1,0:T(8,128)(2,1)S(1)}, bf16[1,4,32,1536]{3,2,1,0:T(8,128)(2,1)S(1)}, ...), condition=%wide.region_1.2_spmd, body=%wide.region_0.1_spmd.sunk | while | flops 638998 | bytes 1868090 | solution.py:103
  15.9 6.1 %collective-permute-done = bf16[1,32,1536]{2,1,0:T(8,128)(2,1)S(1)} collective-permute-done((bf16[1,32,1536]{2,1,0:T(8,128)(2,1)S(1)}, bf16[1,32,1536]{2,1,0:T(8,128)(2,1)S(1)}, u32[]{:S(2)}, u32[]{:S(2)}) %collective-permute-start) | collective-permute-done | bytes 98336 | tf_op jit(solution)/shard_map/while/body/eval_jaxpr/ppermute | solution.py:30
  22.3 6.1 %collective-permute-done = bf16[1,32,1536]{2,1,0:T(8,128)(2,1)S(1)} collective-permute-done((bf16[1,32,1536]{2,1,0:T(8,128)(2,1)S(1)}, bf16[1,32,1536]{2,1,0:T(8,128)(2,1)S(1)}, u32[]{:S(2)}, u32[]{:S(2)}) %collective-permute-start) | collective-permute-done | bytes 98336 | tf_op jit(solution)/shard_map/while/body/eval_jaxpr/ppermute | solution.py:30
  28.8 6.1 %collective-permute-done = bf16[1,32,1536]{2,1,0:T(8,128)(2,1)S(1)} collective-permute-done((bf16[1,32,1536]{2,1,0:T(8,128)(2,1)S(1)}, bf16[1,32,1536]{2,1,0:T(8,128)(2,1)S(1)}, u32[]{:S(2)}, u32[]{:S(2)}) %collective-permute-start) | collective-permute-done | bytes 98336 | tf_op jit(solution)/shard_map/while/body/eval_jaxpr/ppermute | solution.py:30
  35.2 6.1 %collective-permute-done = bf16[1,32,1536]{2,1,0:T(8,128)(2,1)S(1)} collective-permute-done((bf16[1,32,1536]{2,1,0:T(8,128)(2,1)S(1)}, bf16[1,32,1536]{2,1,0:T(8,128)(2,1)S(1)}, u32[]{:S(2)}, u32[]{:S(2)}) %collective-permute-start) | collective-permute-done | bytes 98336 | tf_op jit(solution)/shard_map/while/body/eval_jaxpr/ppermute | solution.py:30
  41.7 6.1 %collective-permute-done = bf16[1,32,1536]{2,1,0:T(8,128)(2,1)S(1)} collective-permute-done((bf16[1,32,1536]{2,1,0:T(8,128)(2,1)S(1)}, bf16[1,32,1536]{2,1,0:T(8,128)(2,1)S(1)}, u32[]{:S(2)}, u32[]{:S(2)}) %collective-permute-start) | collective-permute-done | bytes 98336 | tf_op jit(solution)/shard_map/while/body/eval_jaxpr/ppermute | solution.py:30
  48.1 6.1 %collective-permute-done = bf16[1,32,1536]{2,1,0:T(8,128)(2,1)S(1)} collective-permute-done((bf16[1,32,1536]{2,1,0:T(8,128)(2,1)S(1)}, bf16[1,32,1536]{2,1,0:T(8,128)(2,1)S(1)}, u32[]{:S(2)}, u32[]{:S(2)}) %collective-permute-start) | collective-permute-done | bytes 98336 | tf_op jit(solution)/shard_map/while/body/eval_jaxpr/ppermute | solution.py:30
  54.6 6.1 %collective-permute-done = bf16[1,32,1536]{2,1,0:T(8,128)(2,1)S(1)} collective-permute-done((bf16[1,32,1536]{2,1,0:T(8,128)(2,1)S(1)}, bf16[1,32,1536]{2,1,0:T(8,128)(2,1)S(1)}, u32[]{:S(2)}, u32[]{:S(2)}) %collective-permute-start) | collective-permute-done | bytes 98336 | tf_op jit(solution)/shard_map/while/body/eval_jaxpr/ppermute | solution.py:30
  61.0 6.1 %collective-permute-done = bf16[1,32,1536]{2,1,0:T(8,128)(2,1)S(1)} collective-permute-done((bf16[1,32,1536]{2,1,0:T(8,128)(2,1)S(1)}, bf16[1,32,1536]{2,1,0:T(8,128)(2,1)S(1)}, u32[]{:S(2)}, u32[]{:S(2)}) %collective-permute-start) | collective-permute-done | bytes 98336 | tf_op jit(solution)/shard_map/while/body/eval_jaxpr/ppermute | solution.py:30
  67.4 6.1 %collective-permute-done = bf16[1,32,1536]{2,1,0:T(8,128)(2,1)S(1)} collective-permute-done((bf16[1,32,1536]{2,1,0:T(8,128)(2,1)S(1)}, bf16[1,32,1536]{2,1,0:T(8,128)(2,1)S(1)}, u32[]{:S(2)}, u32[]{:S(2)}) %collective-permute-start) | collective-permute-done | bytes 98336 | tf_op jit(solution)/shard_map/while/body/eval_jaxpr/ppermute | solution.py:30
  73.9 6.1 %collective-permute-done = bf16[1,32,1536]{2,1,0:T(8,128)(2,1)S(1)} collective-permute-done((bf16[1,32,1536]{2,1,0:T(8,128)(2,1)S(1)}, bf16[1,32,1536]{2,1,0:T(8,128)(2,1)S(1)}, u32[]{:S(2)}, u32[]{:S(2)}) %collective-permute-start) | collective-permute-done | bytes 98336 | tf_op jit(solution)/shard_map/while/body/eval_jaxpr/ppermute | solution.py:30
  80.3 6.1 %collective-permute-done = bf16[1,32,1536]{2,1,0:T(8,128)(2,1)S(1)} collective-permute-done((bf16[1,32,1536]{2,1,0:T(8,128)(2,1)S(1)}, bf16[1,32,1536]{2,1,0:T(8,128)(2,1)S(1)}, u32[]{:S(2)}, u32[]{:S(2)}) %collective-permute-start) | collective-permute-done | bytes 98336 | tf_op jit(solution)/shard_map/while/body/eval_jaxpr/ppermute | solution.py:30
  86.8 6.1 %collective-permute-done = bf16[1,32,1536]{2,1,0:T(8,128)(2,1)S(1)} collective-permute-done((bf16[1,32,1536]{2,1,0:T(8,128)(2,1)S(1)}, bf16[1,32,1536]{2,1,0:T(8,128)(2,1)S(1)}, u32[]{:S(2)}, u32[]{:S(2)}) %collective-permute-start) | collective-permute-done | bytes 98336 | tf_op jit(solution)/shard_map/while/body/eval_jaxpr/ppermute | solution.py:30
  93.2 6.1 %collective-permute-done = bf16[1,32,1536]{2,1,0:T(8,128)(2,1)S(1)} collective-permute-done((bf16[1,32,1536]{2,1,0:T(8,128)(2,1)S(1)}, bf16[1,32,1536]{2,1,0:T(8,128)(2,1)S(1)}, u32[]{:S(2)}, u32[]{:S(2)}) %collective-permute-start) | collective-permute-done | bytes 98336 | tf_op jit(solution)/shard_map/while/body/eval_jaxpr/ppermute | solution.py:30
  99.6 6.1 %collective-permute-done = bf16[1,32,1536]{2,1,0:T(8,128)(2,1)S(1)} collective-permute-done((bf16[1,32,1536]{2,1,0:T(8,128)(2,1)S(1)}, bf16[1,32,1536]{2,1,0:T(8,128)(2,1)S(1)}, u32[]{:S(2)}, u32[]{:S(2)}) %collective-permute-start) | collective-permute-done | bytes 98336 | tf_op jit(solution)/shard_map/while/body/eval_jaxpr/ppermute | solution.py:30
  106.1 6.1 %collective-permute-done = bf16[1,32,1536]{2,1,0:T(8,128)(2,1)S(1)} collective-permute-done((bf16[1,32,1536]{2,1,0:T(8,128)(2,1)S(1)}, bf16[1,32,1536]{2,1,0:T(8,128)(2,1)S(1)}, u32[]{:S(2)}, u32[]{:S(2)}) %collective-permute-start) | collective-permute-done | bytes 98336 | tf_op jit(solution)/shard_map/while/body/eval_jaxpr/ppermute | solution.py:30
  112.5 88.9 %while.60 = (s32[]{:T(128)}, bf16[32,1,32,1024]{3,2,1,0:T(8,128)(2,1)}, s32[32,1,4,8]{3,2,1,0:T(4,128)S(1)}, bf16[1,4,32,12,128]{4,2,3,1,0:T(8,128)(2,1)S(1)}, b...) while((s32[]{:T(128)}, ...), condition=%wide.region_5.6_spmd, body=%wide.region_2.5_spmd.sunk | while | flops 34538208 | bytes 5082797 | solution.py:56
  201.4 2.3 fusion.36
  209.9 282.6 %while.62 = (s32[]{:T(128)}, f32[1,4,32,1536]{3,2,1,0:T(8,128)S(1)}, f32[1,32,1024]{2,1,0:T(8,128)S(1)}, s32[32,1,4,8]{3,2,1,0:T(4,128)S(1)}, bf16[32,128,128]{2...) while((s32[]{:T(128)}, ...), condition=%wide.region_13.14_spmd.clone, body=%wide.region_9.13_spmd.clone.sunk | while | flops 69862496 | bytes 23010712 | solution.py:56
  258.9 2.2 scatter_fusion
  285.4 2.2 scatter_fusion
  382.5 2.2 scatter_fusion
  409.0 2.2 scatter_fusion
  417.8 2.2 scatter_fusion
  426.7 2.2 scatter_fusion
  470.8 2.2 scatter_fusion
  493.8 94.3 %while.61 = (s32[]{:T(128)}, f32[1,32,1536]{2,1,0:T(8,128)S(1)}, s32[]{:T(128)}, s32[1,4]{1,0:T(1,128)S(1)}, f32[1,4,32,1536]{3,2,1,0:T(8,128)S(1)}, /*index=5*/...) while((s32[]{:T(128)}, f32[1,32,1536]{2,1,0:T(8,128)S(1)}, s32[]{:T(128)}, s32[1,4]{1,0:T(1,128)S(1)}, ...), condition=%wide.region_15.16_spmd, body=%wide.region_14.15_spmd.sunk | while | flops 2506771 | bytes 2162982 | solution.py:129
  495.3 4.8 collective-permute-done.1
  501.5 4.8 collective-permute-done.1
  507.8 4.8 collective-permute-done.1
  514.1 4.8 collective-permute-done.1
  520.4 4.8 collective-permute-done.1
  526.7 4.8 collective-permute-done.1
  533.0 4.8 collective-permute-done.1
  539.3 4.8 collective-permute-done.1
  545.6 4.8 collective-permute-done.1
  551.8 4.8 collective-permute-done.1
  558.1 4.8 collective-permute-done.1
  564.4 4.8 collective-permute-done.1
  570.7 4.8 collective-permute-done.1
  577.0 4.8 collective-permute-done.1
  583.3 4.8 collective-permute-done.1
  588.2 3.0 collective-permute-start.4
  591.1 4.4 collective-permute-start.5
  595.5 4.8 collective-permute-done.5
  (1872 shorter events, 383.9 us)
Async XLA Ops:
  0.6 8.1 %copy-start = (s32[16,4]{0,1:T(4,128)S(1)}, s32[16,4]{0,1:T(4,128)}, u32[]{:S(2)}) copy-start(s32[16,4]{0,1:T(4,128)} %param.16) | copy-start | bytes 772
  1.4 8.5 %collective-permute-start.2 = (bf16[1,32,256]{2,1,0:T(8,128)(2,1)S(1)}, bf16[1,32,256]{2,1,0:T(8,128)(2,1)S(1)}, u32[]{:S(2)}, u32[]{:S(2)}) collective-permute-start(bf16[1,32,256]{2,1,0:T(8,128)(2,1)S(1)} %get-tuple-element.636), channel_id=1, source_target_pairs={{0,1},{1,2},{2,3},{3,4},{4,5},{5,6},{6,7},{7,8},{8,9},{9,10},{10,1... | collective-permute-start | bytes 49160 | tf_op jit(solution)/shard_map/ppermute | solution.py:18
  6.4 9.2 %collective-permute-start.3 = (bf16[1,32,256]{2,1,0:T(8,128)(2,1)S(1)}, bf16[1,32,256]{2,1,0:T(8,128)(2,1)S(1)}, u32[]{:S(2)}, u32[]{:S(2)}) collective-permute-start(bf16[1,32,256]{2,1,0:T(8,128)(2,1)S(1)} %get-tuple-element.635), channel_id=1, source_target_pairs={{1,0},{2,1},{3,2},{4,3},{5,4},{6,5},{7,6},{8,7},{9,8},{10,9},{11,1... | collective-permute-start | bytes 49160 | tf_op jit(solution)/shard_map/ppermute | solution.py:20
  15.8 6.2 %collective-permute-start = (bf16[1,32,1536]{2,1,0:T(8,128)(2,1)S(1)}, bf16[1,32,1536]{2,1,0:T(8,128)(2,1)S(1)}, u32[]{:S(2)}, u32[]{:S(2)}) collective-permute-start(bf16[1,32,1536]{2,1,0:T(8,128)(2,1)S(1)} %get-tuple-element.816), channel_id=1, source_target_pairs={{240,0},{0,16},{16,32},{32,48},{48,64},{64,80},{80,96},{96,112},{1... | collective-permute-start | bytes 294920 | tf_op jit(solution)/shard_map/while/body/eval_jaxpr/ppermute | solution.py:30
  22.2 6.2 %collective-permute-start = (bf16[1,32,1536]{2,1,0:T(8,128)(2,1)S(1)}, bf16[1,32,1536]{2,1,0:T(8,128)(2,1)S(1)}, u32[]{:S(2)}, u32[]{:S(2)}) collective-permute-start(bf16[1,32,1536]{2,1,0:T(8,128)(2,1)S(1)} %get-tuple-element.816), channel_id=1, source_target_pairs={{240,0},{0,16},{16,32},{32,48},{48,64},{64,80},{80,96},{96,112},{1... | collective-permute-start | bytes 294920 | tf_op jit(solution)/shard_map/while/body/eval_jaxpr/ppermute | solution.py:30
  28.7 6.2 %collective-permute-start = (bf16[1,32,1536]{2,1,0:T(8,128)(2,1)S(1)}, bf16[1,32,1536]{2,1,0:T(8,128)(2,1)S(1)}, u32[]{:S(2)}, u32[]{:S(2)}) collective-permute-start(bf16[1,32,1536]{2,1,0:T(8,128)(2,1)S(1)} %get-tuple-element.816), channel_id=1, source_target_pairs={{240,0},{0,16},{16,32},{32,48},{48,64},{64,80},{80,96},{96,112},{1... | collective-permute-start | bytes 294920 | tf_op jit(solution)/shard_map/while/body/eval_jaxpr/ppermute | solution.py:30
  35.1 6.2 %collective-permute-start = (bf16[1,32,1536]{2,1,0:T(8,128)(2,1)S(1)}, bf16[1,32,1536]{2,1,0:T(8,128)(2,1)S(1)}, u32[]{:S(2)}, u32[]{:S(2)}) collective-permute-start(bf16[1,32,1536]{2,1,0:T(8,128)(2,1)S(1)} %get-tuple-element.816), channel_id=1, source_target_pairs={{240,0},{0,16},{16,32},{32,48},{48,64},{64,80},{80,96},{96,112},{1... | collective-permute-start | bytes 294920 | tf_op jit(solution)/shard_map/while/body/eval_jaxpr/ppermute | solution.py:30
  41.5 6.2 %collective-permute-start = (bf16[1,32,1536]{2,1,0:T(8,128)(2,1)S(1)}, bf16[1,32,1536]{2,1,0:T(8,128)(2,1)S(1)}, u32[]{:S(2)}, u32[]{:S(2)}) collective-permute-start(bf16[1,32,1536]{2,1,0:T(8,128)(2,1)S(1)} %get-tuple-element.816), channel_id=1, source_target_pairs={{240,0},{0,16},{16,32},{32,48},{48,64},{64,80},{80,96},{96,112},{1... | collective-permute-start | bytes 294920 | tf_op jit(solution)/shard_map/while/body/eval_jaxpr/ppermute | solution.py:30
  48.0 6.2 %collective-permute-start = (bf16[1,32,1536]{2,1,0:T(8,128)(2,1)S(1)}, bf16[1,32,1536]{2,1,0:T(8,128)(2,1)S(1)}, u32[]{:S(2)}, u32[]{:S(2)}) collective-permute-start(bf16[1,32,1536]{2,1,0:T(8,128)(2,1)S(1)} %get-tuple-element.816), channel_id=1, source_target_pairs={{240,0},{0,16},{16,32},{32,48},{48,64},{64,80},{80,96},{96,112},{1... | collective-permute-start | bytes 294920 | tf_op jit(solution)/shard_map/while/body/eval_jaxpr/ppermute | solution.py:30
  54.4 6.2 %collective-permute-start = (bf16[1,32,1536]{2,1,0:T(8,128)(2,1)S(1)}, bf16[1,32,1536]{2,1,0:T(8,128)(2,1)S(1)}, u32[]{:S(2)}, u32[]{:S(2)}) collective-permute-start(bf16[1,32,1536]{2,1,0:T(8,128)(2,1)S(1)} %get-tuple-element.816), channel_id=1, source_target_pairs={{240,0},{0,16},{16,32},{32,48},{48,64},{64,80},{80,96},{96,112},{1... | collective-permute-start | bytes 294920 | tf_op jit(solution)/shard_map/while/body/eval_jaxpr/ppermute | solution.py:30
  60.9 6.2 %collective-permute-start = (bf16[1,32,1536]{2,1,0:T(8,128)(2,1)S(1)}, bf16[1,32,1536]{2,1,0:T(8,128)(2,1)S(1)}, u32[]{:S(2)}, u32[]{:S(2)}) collective-permute-start(bf16[1,32,1536]{2,1,0:T(8,128)(2,1)S(1)} %get-tuple-element.816), channel_id=1, source_target_pairs={{240,0},{0,16},{16,32},{32,48},{48,64},{64,80},{80,96},{96,112},{1... | collective-permute-start | bytes 294920 | tf_op jit(solution)/shard_map/while/body/eval_jaxpr/ppermute | solution.py:30
  67.3 6.2 %collective-permute-start = (bf16[1,32,1536]{2,1,0:T(8,128)(2,1)S(1)}, bf16[1,32,1536]{2,1,0:T(8,128)(2,1)S(1)}, u32[]{:S(2)}, u32[]{:S(2)}) collective-permute-start(bf16[1,32,1536]{2,1,0:T(8,128)(2,1)S(1)} %get-tuple-element.816), channel_id=1, source_target_pairs={{240,0},{0,16},{16,32},{32,48},{48,64},{64,80},{80,96},{96,112},{1... | collective-permute-start | bytes 294920 | tf_op jit(solution)/shard_map/while/body/eval_jaxpr/ppermute | solution.py:30
  73.8 6.2 %collective-permute-start = (bf16[1,32,1536]{2,1,0:T(8,128)(2,1)S(1)}, bf16[1,32,1536]{2,1,0:T(8,128)(2,1)S(1)}, u32[]{:S(2)}, u32[]{:S(2)}) collective-permute-start(bf16[1,32,1536]{2,1,0:T(8,128)(2,1)S(1)} %get-tuple-element.816), channel_id=1, source_target_pairs={{240,0},{0,16},{16,32},{32,48},{48,64},{64,80},{80,96},{96,112},{1... | collective-permute-start | bytes 294920 | tf_op jit(solution)/shard_map/while/body/eval_jaxpr/ppermute | solution.py:30
  80.2 6.2 %collective-permute-start = (bf16[1,32,1536]{2,1,0:T(8,128)(2,1)S(1)}, bf16[1,32,1536]{2,1,0:T(8,128)(2,1)S(1)}, u32[]{:S(2)}, u32[]{:S(2)}) collective-permute-start(bf16[1,32,1536]{2,1,0:T(8,128)(2,1)S(1)} %get-tuple-element.816), channel_id=1, source_target_pairs={{240,0},{0,16},{16,32},{32,48},{48,64},{64,80},{80,96},{96,112},{1... | collective-permute-start | bytes 294920 | tf_op jit(solution)/shard_map/while/body/eval_jaxpr/ppermute | solution.py:30
  86.6 6.2 %collective-permute-start = (bf16[1,32,1536]{2,1,0:T(8,128)(2,1)S(1)}, bf16[1,32,1536]{2,1,0:T(8,128)(2,1)S(1)}, u32[]{:S(2)}, u32[]{:S(2)}) collective-permute-start(bf16[1,32,1536]{2,1,0:T(8,128)(2,1)S(1)} %get-tuple-element.816), channel_id=1, source_target_pairs={{240,0},{0,16},{16,32},{32,48},{48,64},{64,80},{80,96},{96,112},{1... | collective-permute-start | bytes 294920 | tf_op jit(solution)/shard_map/while/body/eval_jaxpr/ppermute | solution.py:30
  93.1 6.2 %collective-permute-start = (bf16[1,32,1536]{2,1,0:T(8,128)(2,1)S(1)}, bf16[1,32,1536]{2,1,0:T(8,128)(2,1)S(1)}, u32[]{:S(2)}, u32[]{:S(2)}) collective-permute-start(bf16[1,32,1536]{2,1,0:T(8,128)(2,1)S(1)} %get-tuple-element.816), channel_id=1, source_target_pairs={{240,0},{0,16},{16,32},{32,48},{48,64},{64,80},{80,96},{96,112},{1... | collective-permute-start | bytes 294920 | tf_op jit(solution)/shard_map/while/body/eval_jaxpr/ppermute | solution.py:30
  99.5 6.2 %collective-permute-start = (bf16[1,32,1536]{2,1,0:T(8,128)(2,1)S(1)}, bf16[1,32,1536]{2,1,0:T(8,128)(2,1)S(1)}, u32[]{:S(2)}, u32[]{:S(2)}) collective-permute-start(bf16[1,32,1536]{2,1,0:T(8,128)(2,1)S(1)} %get-tuple-element.816), channel_id=1, source_target_pairs={{240,0},{0,16},{16,32},{32,48},{48,64},{64,80},{80,96},{96,112},{1... | collective-permute-start | bytes 294920 | tf_op jit(solution)/shard_map/while/body/eval_jaxpr/ppermute | solution.py:30
  106.0 6.2 %collective-permute-start = (bf16[1,32,1536]{2,1,0:T(8,128)(2,1)S(1)}, bf16[1,32,1536]{2,1,0:T(8,128)(2,1)S(1)}, u32[]{:S(2)}, u32[]{:S(2)}) collective-permute-start(bf16[1,32,1536]{2,1,0:T(8,128)(2,1)S(1)} %get-tuple-element.816), channel_id=1, source_target_pairs={{240,0},{0,16},{16,32},{32,48},{48,64},{64,80},{80,96},{96,112},{1... | collective-permute-start | bytes 294920 | tf_op jit(solution)/shard_map/while/body/eval_jaxpr/ppermute | solution.py:30
  112.5 88.9 %copy-start.3 = (bf16[3,8,32]{2,1,0:T(8,128)(2,1)S(1)}, bf16[3,8,32]{2,1,0:T(8,128)(2,1)}, u32[]{:S(2)}) copy-start(bf16[3,8,32]{2,1,0:T(8,128)(2,1)} %param.19) | copy-start | bytes 4612
  201.3 2.3 copy-start.2
  204.3 0.9 copy-start.5
  213.5 0.9 copy-start.1
  222.4 0.9 copy-start.1
  231.2 0.9 copy-start.1
  248.9 0.9 copy-start.1
  257.7 0.9 copy-start.1
  266.5 0.9 copy-start.1
  275.4 0.9 copy-start.1
  284.2 0.9 copy-start.1
  301.9 0.9 copy-start.1
  493.8 106.6 %copy-start.6 = (pred[1024]{0:T(1024)(128)(4,1)S(1)}, pred[1024]{0:T(1024)(128)(4,1)}, u32[]{:S(2)}) copy-start(pred[1024]{0:T(1024)(128)(4,1)} %constant.291.clone.1) | copy-start | bytes 3076
  493.9 6.2 %collective-permute-start.1 = (bf16[1,32,1536]{2,1,0:T(8,128)(2,1)S(1)}, bf16[1,32,1536]{2,1,0:T(8,128)(2,1)S(1)}, u32[]{:S(2)}, u32[]{:S(2)}) collective-permute-start(bf16[1,32,1536]{2,1,0:T(8,128)(2,1)S(1)} %convert_element_type.255), channel_id=1, source_target_pairs={{240,0},{0,16},{16,32},{32,48},{48,64},{64,80},{80,96},{96,112},{1... | collective-permute-start | bytes 294920 | tf_op jit(solution)/shard_map/while/body/eval_jaxpr/ppermute | solution.py:30
  500.2 6.2 %collective-permute-start.1 = (bf16[1,32,1536]{2,1,0:T(8,128)(2,1)S(1)}, bf16[1,32,1536]{2,1,0:T(8,128)(2,1)S(1)}, u32[]{:S(2)}, u32[]{:S(2)}) collective-permute-start(bf16[1,32,1536]{2,1,0:T(8,128)(2,1)S(1)} %convert_element_type.255), channel_id=1, source_target_pairs={{240,0},{0,16},{16,32},{32,48},{48,64},{64,80},{80,96},{96,112},{1... | collective-permute-start | bytes 294920 | tf_op jit(solution)/shard_map/while/body/eval_jaxpr/ppermute | solution.py:30
  506.4 6.2 %collective-permute-start.1 = (bf16[1,32,1536]{2,1,0:T(8,128)(2,1)S(1)}, bf16[1,32,1536]{2,1,0:T(8,128)(2,1)S(1)}, u32[]{:S(2)}, u32[]{:S(2)}) collective-permute-start(bf16[1,32,1536]{2,1,0:T(8,128)(2,1)S(1)} %convert_element_type.255), channel_id=1, source_target_pairs={{240,0},{0,16},{16,32},{32,48},{48,64},{64,80},{80,96},{96,112},{1... | collective-permute-start | bytes 294920 | tf_op jit(solution)/shard_map/while/body/eval_jaxpr/ppermute | solution.py:30
  512.7 6.2 %collective-permute-start.1 = (bf16[1,32,1536]{2,1,0:T(8,128)(2,1)S(1)}, bf16[1,32,1536]{2,1,0:T(8,128)(2,1)S(1)}, u32[]{:S(2)}, u32[]{:S(2)}) collective-permute-start(bf16[1,32,1536]{2,1,0:T(8,128)(2,1)S(1)} %convert_element_type.255), channel_id=1, source_target_pairs={{240,0},{0,16},{16,32},{32,48},{48,64},{64,80},{80,96},{96,112},{1... | collective-permute-start | bytes 294920 | tf_op jit(solution)/shard_map/while/body/eval_jaxpr/ppermute | solution.py:30
  519.0 6.2 %collective-permute-start.1 = (bf16[1,32,1536]{2,1,0:T(8,128)(2,1)S(1)}, bf16[1,32,1536]{2,1,0:T(8,128)(2,1)S(1)}, u32[]{:S(2)}, u32[]{:S(2)}) collective-permute-start(bf16[1,32,1536]{2,1,0:T(8,128)(2,1)S(1)} %convert_element_type.255), channel_id=1, source_target_pairs={{240,0},{0,16},{16,32},{32,48},{48,64},{64,80},{80,96},{96,112},{1... | collective-permute-start | bytes 294920 | tf_op jit(solution)/shard_map/while/body/eval_jaxpr/ppermute | solution.py:30
  525.3 6.2 %collective-permute-start.1 = (bf16[1,32,1536]{2,1,0:T(8,128)(2,1)S(1)}, bf16[1,32,1536]{2,1,0:T(8,128)(2,1)S(1)}, u32[]{:S(2)}, u32[]{:S(2)}) collective-permute-start(bf16[1,32,1536]{2,1,0:T(8,128)(2,1)S(1)} %convert_element_type.255), channel_id=1, source_target_pairs={{240,0},{0,16},{16,32},{32,48},{48,64},{64,80},{80,96},{96,112},{1... | collective-permute-start | bytes 294920 | tf_op jit(solution)/shard_map/while/body/eval_jaxpr/ppermute | solution.py:30
  531.6 6.2 %collective-permute-start.1 = (bf16[1,32,1536]{2,1,0:T(8,128)(2,1)S(1)}, bf16[1,32,1536]{2,1,0:T(8,128)(2,1)S(1)}, u32[]{:S(2)}, u32[]{:S(2)}) collective-permute-start(bf16[1,32,1536]{2,1,0:T(8,128)(2,1)S(1)} %convert_element_type.255), channel_id=1, source_target_pairs={{240,0},{0,16},{16,32},{32,48},{48,64},{64,80},{80,96},{96,112},{1... | collective-permute-start | bytes 294920 | tf_op jit(solution)/shard_map/while/body/eval_jaxpr/ppermute | solution.py:30
  537.9 6.2 %collective-permute-start.1 = (bf16[1,32,1536]{2,1,0:T(8,128)(2,1)S(1)}, bf16[1,32,1536]{2,1,0:T(8,128)(2,1)S(1)}, u32[]{:S(2)}, u32[]{:S(2)}) collective-permute-start(bf16[1,32,1536]{2,1,0:T(8,128)(2,1)S(1)} %convert_element_type.255), channel_id=1, source_target_pairs={{240,0},{0,16},{16,32},{32,48},{48,64},{64,80},{80,96},{96,112},{1... | collective-permute-start | bytes 294920 | tf_op jit(solution)/shard_map/while/body/eval_jaxpr/ppermute | solution.py:30
  544.2 6.2 %collective-permute-start.1 = (bf16[1,32,1536]{2,1,0:T(8,128)(2,1)S(1)}, bf16[1,32,1536]{2,1,0:T(8,128)(2,1)S(1)}, u32[]{:S(2)}, u32[]{:S(2)}) collective-permute-start(bf16[1,32,1536]{2,1,0:T(8,128)(2,1)S(1)} %convert_element_type.255), channel_id=1, source_target_pairs={{240,0},{0,16},{16,32},{32,48},{48,64},{64,80},{80,96},{96,112},{1... | collective-permute-start | bytes 294920 | tf_op jit(solution)/shard_map/while/body/eval_jaxpr/ppermute | solution.py:30
  550.5 6.2 %collective-permute-start.1 = (bf16[1,32,1536]{2,1,0:T(8,128)(2,1)S(1)}, bf16[1,32,1536]{2,1,0:T(8,128)(2,1)S(1)}, u32[]{:S(2)}, u32[]{:S(2)}) collective-permute-start(bf16[1,32,1536]{2,1,0:T(8,128)(2,1)S(1)} %convert_element_type.255), channel_id=1, source_target_pairs={{240,0},{0,16},{16,32},{32,48},{48,64},{64,80},{80,96},{96,112},{1... | collective-permute-start | bytes 294920 | tf_op jit(solution)/shard_map/while/body/eval_jaxpr/ppermute | solution.py:30
  556.7 6.2 %collective-permute-start.1 = (bf16[1,32,1536]{2,1,0:T(8,128)(2,1)S(1)}, bf16[1,32,1536]{2,1,0:T(8,128)(2,1)S(1)}, u32[]{:S(2)}, u32[]{:S(2)}) collective-permute-start(bf16[1,32,1536]{2,1,0:T(8,128)(2,1)S(1)} %convert_element_type.255), channel_id=1, source_target_pairs={{240,0},{0,16},{16,32},{32,48},{48,64},{64,80},{80,96},{96,112},{1... | collective-permute-start | bytes 294920 | tf_op jit(solution)/shard_map/while/body/eval_jaxpr/ppermute | solution.py:30
  563.0 6.2 %collective-permute-start.1 = (bf16[1,32,1536]{2,1,0:T(8,128)(2,1)S(1)}, bf16[1,32,1536]{2,1,0:T(8,128)(2,1)S(1)}, u32[]{:S(2)}, u32[]{:S(2)}) collective-permute-start(bf16[1,32,1536]{2,1,0:T(8,128)(2,1)S(1)} %convert_element_type.255), channel_id=1, source_target_pairs={{240,0},{0,16},{16,32},{32,48},{48,64},{64,80},{80,96},{96,112},{1... | collective-permute-start | bytes 294920 | tf_op jit(solution)/shard_map/while/body/eval_jaxpr/ppermute | solution.py:30
  569.3 6.2 %collective-permute-start.1 = (bf16[1,32,1536]{2,1,0:T(8,128)(2,1)S(1)}, bf16[1,32,1536]{2,1,0:T(8,128)(2,1)S(1)}, u32[]{:S(2)}, u32[]{:S(2)}) collective-permute-start(bf16[1,32,1536]{2,1,0:T(8,128)(2,1)S(1)} %convert_element_type.255), channel_id=1, source_target_pairs={{240,0},{0,16},{16,32},{32,48},{48,64},{64,80},{80,96},{96,112},{1... | collective-permute-start | bytes 294920 | tf_op jit(solution)/shard_map/while/body/eval_jaxpr/ppermute | solution.py:30
  575.6 6.2 %collective-permute-start.1 = (bf16[1,32,1536]{2,1,0:T(8,128)(2,1)S(1)}, bf16[1,32,1536]{2,1,0:T(8,128)(2,1)S(1)}, u32[]{:S(2)}, u32[]{:S(2)}) collective-permute-start(bf16[1,32,1536]{2,1,0:T(8,128)(2,1)S(1)} %convert_element_type.255), channel_id=1, source_target_pairs={{240,0},{0,16},{16,32},{32,48},{48,64},{64,80},{80,96},{96,112},{1... | collective-permute-start | bytes 294920 | tf_op jit(solution)/shard_map/while/body/eval_jaxpr/ppermute | solution.py:30
  581.9 6.2 %collective-permute-start.1 = (bf16[1,32,1536]{2,1,0:T(8,128)(2,1)S(1)}, bf16[1,32,1536]{2,1,0:T(8,128)(2,1)S(1)}, u32[]{:S(2)}, u32[]{:S(2)}) collective-permute-start(bf16[1,32,1536]{2,1,0:T(8,128)(2,1)S(1)} %convert_element_type.255), channel_id=1, source_target_pairs={{240,0},{0,16},{16,32},{32,48},{48,64},{64,80},{80,96},{96,112},{1... | collective-permute-start | bytes 294920 | tf_op jit(solution)/shard_map/while/body/eval_jaxpr/ppermute | solution.py:30
  588.2 7.4 %collective-permute-start.4 = (bf16[1,32,256]{2,1,0:T(8,128)(2,1)S(1)}, bf16[1,32,256]{2,1,0:T(8,128)(2,1)S(1)}, u32[]{:S(2)}, u32[]{:S(2)}) collective-permute-start(bf16[1,32,256]{2,1,0:T(8,128)(2,1)S(1)} %get-tuple-element.630), channel_id=1, source_target_pairs={{0,1},{1,2},{2,3},{3,4},{4,5},{5,6},{6,7},{7,8},{8,9},{9,10},{10,1... | collective-permute-start | bytes 49160 | tf_op jit(solution)/shard_map/ppermute | solution.py:18
  591.1 9.2 %collective-permute-start.5 = (bf16[1,32,256]{2,1,0:T(8,128)(2,1)S(1)}, bf16[1,32,256]{2,1,0:T(8,128)(2,1)S(1)}, u32[]{:S(2)}, u32[]{:S(2)}) collective-permute-start(bf16[1,32,256]{2,1,0:T(8,128)(2,1)S(1)} %get-tuple-element.631), channel_id=1, source_target_pairs={{1,0},{2,1},{3,2},{4,3},{5,4},{6,5},{7,6},{8,7},{9,8},{10,9},{11,1... | collective-permute-start | bytes 49160 | tf_op jit(solution)/shard_map/ppermute | solution.py:20
  (24 other events, 20.3 us)
where the time goes:
time: 608 us; the launch traced here: 601 us
  waiting for transfers between devices  174 us (29%)
  other arithmetic  167 us (27%)
  local copies, waits for them, and re-layouts  162 us (27%)
  matrix products  70.8 us (12%)
  starting transfers between devices  17.2 us (3%)
  loops' own time  10.3 us (2%)
    ppermute x30, waiting for transfers between devices, passed_along(): return lax.ppermute(block, axis, route)  164 us
    scatter-add x96, other arithmetic, warp_block(): jnp.take(blockset, where_at, axis=1)  72.9 us
    squeeze x96, local copies, waits for them, and re-layouts, local_depth(): volume = lax.map(jax.checkpoint(per_plane), (plane_index, kernels))  51.5 us
    gather x128, local copies, waits for them, and re-layouts, warp_block(): jnp.take(blockset, where_at, axis=1)  48.3 us
    dot_general x96, matrix products, warp_block(): jnp.dot(picked.reshape(-1, 128), kernel, preferred_element_type=jnp.float32)  44.6 us
    add_any x64, other arithmetic, local_depth(): volume = lax.map(jax.checkpoint(per_plane), (plane_index, kernels))  38.5 us
    dynamic_update_slice x32, other arithmetic, local_depth(): volume = lax.map(jax.checkpoint(per_plane), (plane_index, kernels))  20.6 us
    dot_general x16, matrix products, contribution(): jnp.einsum('ajk,ajcp->kcp', matches.astype(jnp.float32), src_grad, precis...  20.3 us
  transfers between devices with their start and end apart: 34, of which 32 were waited for; matrix products, arithmetic and copies ran while one was open for 4% of the time, Pallas kernels for 0%

commit v1 on v0

v1 whole, which is shorter than its diff:
```python
import functools

import jax
import jax.numpy as jnp
from jax import lax
from jax.experimental import pallas as pl
from jax.experimental.pallas import tpu as pltpu
from jax.sharding import PartitionSpec as P

MESH = pl.DeviceIdType.MESH
f32, bf16, i32 = jnp.float32, jnp.bfloat16, jnp.int32

C = 32
D = 32
V = 4
NF = 8
NB = 8
W = 5
ZERO = 2 * NF * W

PARTS = ((0, 0, 2, 3), (1, 1, 1, 4), (2, 5, 0, 5), (6, 6, 0, 4), (7, 7, 0, 3))


def place():
    frame = lax.axis_index("frame")
    tile = lax.axis_index("tile")
    core = frame % 2
    own = frame // 2
    return frame, core, own, (own % 4) * 2 + own // 4, tile, lax.axis_size("tile")


def frame_at(block, core):
    return (block % 2) * 8 + (block // 2) * 2 + core


def signal(semaphore, frame, tile):
    pl.semaphore_signal(semaphore, inc=1, device_id=(frame, tile), device_id_type=MESH)


def remote(src, dst, send, recv, frame, tile):
    return pltpu.make_async_remote_copy(
        src_ref=src, dst_ref=dst, send_sem=send, recv_sem=recv, device_id=(frame, tile), device_id_type=MESH
    )


def wait_bytes(ref, semaphore):
    pltpu.make_async_copy(ref, ref, semaphore).wait()


def exchange_kernel(
    feats, offsets, cot, views, win, index_out, cot_out,
    blocks, aux, aux_rx, send, recv, aux_send, aux_recv, rim_send, sib_send, sib_recv,
):
    frame, core, own, mine, tile, tiles = place()
    before, after = (tile + tiles - 1) % tiles, (tile + 1) % tiles
    sibling = frame + 1 - 2 * core

    barrier = pltpu.get_barrier_semaphore()

    def greet(s, carry):
        signal(barrier, frame_at((mine + s) % NB, core), tile)
        return carry

    lax.fori_loop(1, NB, greet, 0)

    @pl.when(mine < 2)
    def _():
        def greet_before(b, carry):
            signal(barrier, frame_at(b, core), before)
            return carry

        lax.fori_loop(0, NB, greet_before, 0)

    @pl.when(mine > 5)
    def _():
        def greet_after(b, carry):
            signal(barrier, frame_at(b, core), after)
            return carry

        lax.fori_loop(0, NB, greet_after, 0)

    signal(barrier, sibling, tile)

    for b in range(NB):
        blocks[b] = feats[:, b * 128:(b + 1) * 128]
        for j in range(V):
            aux[b, :, j * D:(j + 1) * D] = offsets[j, b:b + 1, :].astype(f32)
        aux[b, :, 128:256] = cot[:, b * 128:(b + 1) * 128]
    win[ZERO] = jnp.zeros((C, 128), bf16)

    pl.semaphore_wait(barrier, 7 + 4 + 1)

    rims = (
        (0, 1, 4, 6, before), (0, 2, 3, 7, before),
        (6, 2, 0, 0, after), (7, 1, 0, 1, after),
    )
    rim_copies = [
        remote(
            blocks.at[pl.ds(first, count)], win.at[pl.ds(own * W + at, count)],
            rim_send.at[n], recv.at[own], frame_at(b, core), where,
        )
        for n, (first, count, at, b, where) in enumerate(rims)
    ]
    for copy in rim_copies:
        copy.start()

    def part_copy(b, at, count):
        return remote(
            blocks.at[pl.ds(b - 2 + at, count)], win.at[pl.ds(own * W + at, count)],
            send.at[b], recv.at[own], frame_at(b, core), tile,
        )

    def aux_copy(b):
        return remote(aux.at[b], aux_rx.at[own], aux_send.at[b], aux_recv.at[own], frame_at(b, core), tile)

    def start(s, carry):
        b = (mine + s) % NB
        aux_copy(b).start()
        for least, most, at, count in PARTS:
            @pl.when((b >= least) & (b <= most))
            def _():
                part_copy(b, at, count).start()
        return carry

    lax.fori_loop(1, NB, start, 0)
    pltpu.make_async_copy(aux.at[mine], aux_rx.at[own], aux_recv.at[own]).start()
    for least, most, at, count in PARTS:
        @pl.when((mine >= least) & (mine <= most))
        def _():
            pltpu.make_async_copy(
                blocks.at[pl.ds(mine - 2 + at, count)], win.at[pl.ds(own * W + at, count)], recv.at[own]
            ).start()

    def window(i):
        return win.at[pl.ds(i * W, W)]

    def to_sibling(i):
        return remote(
            window(i), window(NF + i), sib_send.at[i], sib_recv.at[i], sibling, tile
        )

    def forward(s, carry):
        i = (own + s) % NF
        wait_bytes(window(i), recv.at[i])
        to_sibling(i).start()
        return carry

    lax.fori_loop(0, NF, forward, 0)

    view_of = lax.broadcasted_iota(i32, (1, 128), 1) // D
    here = tile * NB + mine
    for i in range(NF):
        wait_bytes(aux_rx.at[i], aux_recv.at[i])
        shift = aux_rx[i, :, 0:128].astype(i32)
        at = here + shift
        row = jnp.zeros((1, 128), i32)
        for j in range(V):
            v = views[j, 2 * i + core]
            row = jnp.where(view_of == j, jnp.where(v % 2 == core, 0, NF * W) + (v // 2) * W + 2, row)
        index_out[i:i + 1, :] = jnp.where((at >= 0) & (at < tiles * NB), row + shift, ZERO)
        cot_out[i:i + 1, :] = aux_rx[i, :, 128:256]

    def settle(s, carry):
        b = (mine + s) % NB
        aux_copy(b).wait_send()
        for least, most, at, count in PARTS:
            @pl.when((b >= least) & (b <= most))
            def _():
                part_copy(b, at, count).wait_send()
        return carry

    lax.fori_loop(1, NB, settle, 0)
    for copy in rim_copies:
        copy.wait_send()

    def settle_sibling(i, carry):
        to_sibling(i).wait_send()
        wait_bytes(window(NF + i), sib_recv.at[i])
        return carry

    lax.fori_loop(0, NF, settle_sibling, 0)


def compute_kernel(
    idx, head, win, ker, reg, cot, depth_out, grad_own, grad_sib, cen, vd, acc_a, acc_b, ref_acc
):
    step = 2
    rows = []
    for t in range(3):
        taps = reg[t].astype(f32)
        rows.append(sum(head[r] * taps[r:r + 1, :] for r in range(8)))
    row_id = lax.broadcasted_iota(i32, (8, C), 0)
    weight = jnp.where(row_id == 0, rows[0], jnp.where(row_id == 1, rows[1], jnp.where(row_id == 2, rows[2], 0.0)))
    w_hi = weight.astype(bf16)
    w_lo = (weight - w_hi.astype(f32)).astype(bf16)
    wide_lane = lax.broadcasted_iota(i32, (C, D * C), 1)
    wide_row = lax.broadcasted_iota(i32, (C, D * C), 0)
    spread = (wide_lane % C == wide_row).astype(f32).astype(bf16)
    tap_of = wide_lane // C - wide_row + 1
    bands = []
    for part in (w_hi, w_lo):
        wide = jnp.dot(part, spread, preferred_element_type=f32)
        bands.append(sum(jnp.where(tap_of == t, wide[t:t + 1, :], 0.0) for t in range(3)))
    mean_of = 1.0 / (V + 1)

    def forward(d, carry):
        mat = ker[d]
        for i0 in range(0, NF, step):
            picks = [win[idx[i, j * D + d]] for i in range(i0, i0 + step) for j in range(V)]
            y = jnp.dot(jnp.concatenate(picks, axis=0), mat, preferred_element_type=f32)
            for i in range(i0, i0 + step):
                o = (i - i0) * V * C
                xs = [win[i * W + 2].astype(f32)] + [y[o + j * C:o + (j + 1) * C] for j in range(V)]
                average = (((xs[0] + xs[1]) + (xs[2] + xs[3])) + xs[4]) * mean_of
                cs = [x - average for x in xs]
                sq = [c * c for c in cs]
                variance = (((sq[0] + sq[1]) + (sq[2] + sq[3])) + sq[4]) * mean_of
                vd[pl.ds(pl.multiple_of(d * C, C), C), i * 128:(i + 1) * 128] = variance.astype(bf16)
                for j in range(V + 1):
                    cen[d, i, j] = cs[j].astype(bf16)
        return carry

    lax.fori_loop(0, D, forward, 0)

    band = jnp.concatenate(bands, axis=0).astype(bf16)
    band_t = jnp.transpose(jnp.concatenate(bands + bands, axis=0)).astype(bf16)
    value = (lax.broadcasted_iota(i32, (D, 128), 0).astype(f32) + 1.0) / D
    for i0 in range(0, NF, 2):
        both = jnp.dot(band, vd[:, i0 * 128:(i0 + 2) * 128], preferred_element_type=f32)
        parts = []
        for i in range(i0, i0 + 2):
            o = (i - i0) * 128
            th = jnp.tanh(both[:D, o:o + 128] + both[D:, o:o + 128])
            w = jnp.exp(4.0 * th)
            total = jnp.sum(w, axis=0, keepdims=True)
            depth = jnp.sum(w * value, axis=0, keepdims=True) / total
            depth_out[i:i + 1, :] = depth
            scale = cot[i:i + 1, :] / total * (4.0 * 2.0 / (V + 1))
            d_pre = (w * (value - depth)) * scale * (1.0 - th * th)
            hi = d_pre.astype(bf16)
            lo = (d_pre - hi.astype(f32)).astype(bf16)
            parts.append(jnp.concatenate([hi, hi, lo, lo], axis=0))
        rhs = jnp.concatenate(parts, axis=1)
        vd[:, i0 * 128:(i0 + 2) * 128] = jnp.dot(band_t, rhs, preferred_element_type=f32).astype(bf16)

    acc_a[...] = jnp.zeros_like(acc_a)
    acc_b[...] = jnp.zeros_like(acc_b)
    ref_acc[...] = jnp.zeros_like(ref_acc)

    def backward(d, carry):
        mat = ker[d]
        for i0 in range(0, NF, step):
            gs = []
            for i in range(i0, i0 + step):
                dv = vd[pl.ds(pl.multiple_of(d * C, C), C), i * 128:(i + 1) * 128]
                ref_acc[i] += (dv * cen[d, i, 0]).astype(f32)
                for j in range(V):
                    gs.append(dv * cen[d, i, j + 1])
            y = lax.dot_general(
                jnp.concatenate(gs, axis=0), mat, (((1,), (1,)), ((), ())), preferred_element_type=f32
            )
            for i in range(i0, i0 + step):
                acc = acc_a if i % 2 == 0 else acc_b
                slots = [idx[i, j * D + d] for j in range(V)]
                o = (i - i0) * V * C
                new = [acc[slots[j]] + y[o + j * C:o + (j + 1) * C] for j in range(V)]
                for j in range(V):
                    acc[slots[j]] = new[j]
        return carry

    lax.fori_loop(0, D, backward, 0)

    for i in range(NF):
        for k in range(W):
            s = i * W + k
            total = acc_a[s] + acc_b[s]
            grad_own[s] = total + ref_acc[i] if k == 2 else total
            grad_sib[s] = (acc_a[NF * W + s] + acc_b[NF * W + s]).astype(bf16)


def return_kernel(
    grad_own, grad_sib, depth, depth_out, grad_out,
    sib_rx, out, depths, depth_rx, rx, send, recv, rim_send, depth_send, depth_recv, sib_send, sib_recv,
):
    frame, core, own, mine, tile, tiles = place()
    before, after = (tile + tiles - 1) % tiles, (tile + 1) % tiles
    sibling = frame + 1 - 2 * core

    barrier = pltpu.get_barrier_semaphore()
    signal(barrier, sibling, tile)

    def greet(s, carry):
        signal(barrier, frame_at((mine + s) % NB, core), tile)
        return carry

    lax.fori_loop(1, NB, greet, 0)
    for b, where in ((6, before), (7, before), (0, after), (1, after)):
        signal(barrier, frame_at(b, core), where)
    for i in range(NF):
        depths[i] = depth[i:i + 1, :]

    pl.semaphore_wait(barrier, jnp.where((mine < 2) | (mine > 5), 2 * NB, NB))

    def window(ref, i):
        return ref.at[pl.ds(i * W, W)]

    def to_sibling(i):
        return remote(
            window(grad_sib, i), window(sib_rx, i), sib_send.at[i], sib_recv.at[i], sibling, tile
        )

    def start_sibling(s, carry):
        to_sibling((own + s) % NF).start()
        return carry

    lax.fori_loop(1, NF + 1, start_sibling, 0)

    def part_copy(i, at, count):
        return remote(
            out.at[pl.ds(i * W + at, count)], rx.at[mine + 2, pl.ds(at, count)],
            send.at[i], recv.at[mine + 2], 2 * i + core, tile,
        )

    def rim_copy(i, at, count, slot, where):
        return remote(
            out.at[pl.ds(i * W + at, count)], rx.at[slot, pl.ds(at, count)],
            rim_send.at[i], recv.at[slot], 2 * i + core, where,
        )

    def depth_copy(i):
        return remote(
            depths.at[i], depth_rx.at[mine], depth_send.at[i], depth_recv.at[mine], 2 * i + core, tile
        )

    rims = ((0, 0, 2, 10, before), (1, 0, 1, 11, before), (6, 4, 1, 0, after), (7, 3, 2, 1, after))

    def add_and_send(s, carry):
        i = (own + s) % NF
        wait_bytes(window(sib_rx, i), sib_recv.at[i])
        for k in range(W):
            out[i * W + k] = (grad_own[i * W + k] + sib_rx[i * W + k].astype(f32)).astype(bf16)
        for b, at, count, slot, where in rims:
            @pl.when(mine == b)
            def _():
                rim_copy(i, at, count, slot, where).start()

        @pl.when(i != own)
        def _():
            depth_copy(i).start()
            for least, most, at, count in PARTS:
                @pl.when((mine >= least) & (mine <= most))
                def _():
                    part_copy(i, at, count).start()

        return carry

    lax.fori_loop(1, NF + 1, add_and_send, 0)
    pltpu.make_async_copy(depths.at[own], depth_rx.at[mine], depth_recv.at[mine]).start()
    for least, most, at, count in PARTS:
        @pl.when((mine >= least) & (mine <= most))
        def _():
            pltpu.make_async_copy(
                out.at[pl.ds(own * W + at, count)], rx.at[mine + 2, pl.ds(at, count)], recv.at[mine + 2]
            ).start()

    for b in range(NB):
        wait_bytes(depth_rx.at[b], depth_recv.at[b])
        depth_out[:, b * 128:(b + 1) * 128] = depth_rx[b]
    for slot in range(NB + 4):
        first, last = max(slot - 4, 0), min(slot, NB - 1)
        wait_bytes(rx.at[slot, pl.ds(first - slot + 4, last - first + 1)], recv.at[slot])
    for b in range(NB):
        total = rx[b, 4].astype(f32)
        for k in range(1, W):
            total += rx[b + k, 4 - k].astype(f32)
        grad_out[:, b * 128:(b + 1) * 128] = total

    def settle(s, carry):
        i = (own + s) % NF
        to_sibling(i).wait_send()
        for b, at, count, slot, where in rims:
            @pl.when(mine == b)
            def _():
                rim_copy(i, at, count, slot, where).wait_send()

        @pl.when(i != own)
        def _():
            depth_copy(i).wait_send()
            for least, most, at, count in PARTS:
                @pl.when((mine >= least) & (mine <= most))
                def _():
                    part_copy(i, at, count).wait_send()

        return carry

    lax.fori_loop(1, NF + 1, settle, 0)


def per_device(features, views, offsets, kernels, reg_weight, head_weight, depth_cot):
    vmem = pl.BlockSpec(memory_space=pltpu.VMEM)
    smem = pl.BlockSpec(memory_space=pltpu.SMEM)
    dma = pltpu.SemaphoreType.DMA
    shape = jax.ShapeDtypeStruct

    win, index, cot = pl.pallas_call(
        exchange_kernel,
        name="exchange",
        out_shape=(shape((ZERO + 1, C, 128), bf16), shape((NF, 128), i32), shape((NF, 128), f32)),
        in_specs=[vmem, vmem, vmem, smem],
        out_specs=(vmem,) * 3,
        scratch_shapes=[
            pltpu.VMEM((NB, C, 128), bf16),
            pltpu.VMEM((NB, 1, 256), f32),
            pltpu.VMEM((NF, 1, 256), f32),
            dma((NB,)), dma((NF,)), dma((NB,)), dma((NF,)), dma((4,)), dma((NF,)), dma((NF,)),
        ],
        compiler_params=pltpu.CompilerParams(
            collective_id=0, has_side_effects=True, vmem_limit_bytes=16 << 20
        ),
    )(features.reshape(C, NB * 128), jnp.transpose(offsets[0], (0, 2, 1)), depth_cot, views.T)

    depth, grad_own, grad_sib = pl.pallas_call(
        compute_kernel,
        name="compute",
        out_shape=(shape((NF, 128), f32), shape((NF * W, C, 128), f32), shape((NF * W, C, 128), bf16)),
        in_specs=[smem, smem, vmem, vmem, vmem, vmem],
        out_specs=(vmem,) * 3,
        scratch_shapes=[
            pltpu.VMEM((D, NF, V + 1, C, 128), bf16),
            pltpu.VMEM((D * C, NF * 128), bf16),
            pltpu.VMEM((ZERO + 1, C, 128), f32),
            pltpu.VMEM((ZERO + 1, C, 128), f32),
            pltpu.VMEM((NF, C, 128), f32),
        ],
        compiler_params=pltpu.CompilerParams(vmem_limit_bytes=40 << 20),
    )(index, head_weight, win, kernels, reg_weight, cot)

    depth_map, grad = pl.pallas_call(
        return_kernel,
        name="give_back",
        out_shape=(shape((1, NB * 128), f32), shape((C, NB * 128), f32)),
        in_specs=[vmem] * 3,
        out_specs=(vmem,) * 2,
        scratch_shapes=[
            pltpu.VMEM((NF * W, C, 128), bf16),
            pltpu.VMEM((NF * W, C, 128), bf16),
            pltpu.VMEM((NF, 1, 128), f32),
            pltpu.VMEM((NB, 1, 128), f32),
            pltpu.VMEM((NB + 4, W, C, 128), bf16),
            dma((NF,)), dma((NB + 4,)), dma((NF,)), dma((NF,)), dma((NB,)), dma((NF,)), dma((NF,)),
        ],
        compiler_params=pltpu.CompilerParams(
            collective_id=1, has_side_effects=True, vmem_limit_bytes=16 << 20
        ),
    )(grad_own, grad_sib, depth)
    return depth_map, grad.reshape(1, C, NB * 128)


def solution(mesh):
    return jax.shard_map(
        per_device,
        mesh=mesh,
        in_specs=(
            P("frame", None, "tile"),
            P(),
            P("frame", None, None, "tile"),
            P(),
            P(),
            P(),
            P("frame", "tile"),
        ),
        out_specs=(P("frame", "tile"), P("frame", None, "tile")),
        check_vma=False,
    )
```

time: 608 us -> 57.3 us (0.09)
  the two profiles are of different devices: /device:TPU:100 before, /device:TPU:1 now
where the time goes in v1:
time: 57.3 us; the launch traced here: 57 us
  Pallas kernels  50.3 us (88%)
  local copies, waits for them, and re-layouts  6.04 us (11%)
  between operations  0.68 us (1%)
    pallas_call x1, Pallas kernels, per_device(): pl.pallas_call(exchange_kernel, name='exchange', out_shape=(shape((ZERO +...  19.7 us
    pallas_call x1, Pallas kernels, per_device(): pl.pallas_call(compute_kernel, name='compute', out_shape=(shape((NF, 128)...  19.2 us
    pallas_call x1, Pallas kernels, per_device(): pl.pallas_call(return_kernel, name='give_back', out_shape=(shape((1, NB *...  11.4 us
    unnamed x16, local copies, waits for them, and re-layouts  6.04 us

profile of v1, /device:TPU:1, one launch (start us, length us, event | category | flops | bytes accessed | tf_op | source)
XLA Modules:
  0.0 57.0 jit_solution(11519086701257112173)
XLA Ops:
  0.6 0.0 copy-start.4
  0.6 0.7 %copy-done.4 = f32[1,1024]{1,0:T(1,128)S(1)} copy-done((f32[1,1024]{1,0:T(1,128)S(1)}, f32[1,1024]{1,0:T(1,128)}, u32[]{:S(2)}) %copy-start.4) | copy-done | bytes 4120
  1.3 0.0 copy-start.1
  1.3 0.8 %copy-done.1 = bf16[1,32,1024]{2,1,0:T(8,128)(2,1)S(1)} copy-done((bf16[1,32,1024]{2,1,0:T(8,128)(2,1)S(1)}, bf16[1,32,1024]{2,1,0:T(8,128)(2,1)}, u32[]{:S(2)}) %copy-start.1) | copy-done | bytes 65560
  2.2 0.0 copy-start.2
  2.2 0.7 %copy-done.2 = s32[1,4,32,8]{2,3,1,0:T(8,128)S(1)} copy-done((s32[1,4,32,8]{2,3,1,0:T(8,128)S(1)}, s32[1,4,32,8]{2,3,1,0:T(8,128)}, u32[]{:S(2)}) %copy-start.2) | copy-done | bytes 4120
  2.9 0.0 copy-start.5
  2.9 0.7 %copy-done.5 = s32[16,4]{0,1:T(4,128)S(1)} copy-done((s32[16,4]{0,1:T(4,128)S(1)}, s32[16,4]{0,1:T(4,128)}, u32[]{:S(2)}) %copy-start.5) | copy-done | bytes 280
  3.6 0.0 copy-start.3
  3.6 19.7 %exchange.1 = (bf16[81,32,128]{2,1,0:T(8,128)(2,1)S(1)}, s32[8,128]{1,0:T(8,128)S(1)}, f32[8,128]{1,0:T(8,128)S(1)}) custom-call(bf16[32,1024]{1,0:T(8,128)(2,1)S(1)} %bitcast.7, s32[4,8,32]{2,1,0:T(8,128)S(1)} %bitcast.8, f32[1,1024]{1,0:T(1,128)S(1)} %copy-done.4, s32[4,16]{1,0:T(4,128)S(1)} %bitcast.9), custom_call_target="tpu_custom_call" | custom-call | tf_op jit(solution)/shard_map/exchange/pallas_call | solution.py:405
  23.3 0.0 copy-start.6
  23.3 0.0 copy-done.3
  23.3 0.6 %copy-done.6 = f32[8]{0:T(128)S(1)} copy-done((f32[8]{0:T(128)S(1)}, f32[8]{0:T(128)}, u32[]{:S(2)}) %copy-start.6) | copy-done | bytes 56
  24.0 0.0 copy-start
  24.0 1.2 %copy-done = bf16[32,128,128]{2,1,0:T(8,128)(2,1)S(1)} copy-done((bf16[32,128,128]{2,1,0:T(8,128)(2,1)S(1)}, bf16[32,128,128]{2,1,0:T(8,128)(2,1)}, u32[]{:S(2)}) %copy-start) | copy-done | bytes 1048600
  25.2 19.2 %compute.1 = (f32[8,128]{1,0:T(8,128)S(1)}, f32[40,32,128]{2,1,0:T(8,128)S(1)}, bf16[40,32,128]{2,1,0:T(8,128)(2,1)S(1)}) custom-call(s32[8,128]{1,0:T(8,128)S(1)} %get-tuple-element.10.idx, f32[8]{0:T(128)S(1)} %copy-done.6, bf16[81,32,128]{2,1,0:T(8,128)(2,1)S(1)} %get-tuple-element.11.win, bf16[32,128,128]{2,1,0:T(8,128)(2,1)S(1)} %copy-done, ...), custom_call_target="tpu_custom_call" | custom-call | tf_op jit(solution)/shard_map/compute/pallas_call | solution.py:422
  44.4 11.4 %give_back.1 = (f32[1,1024]{1,0:T(1,128)S(1)}, f32[32,1024]{1,0:T(8,128)S(1)}) custom-call(f32[40,32,128]{2,1,0:T(8,128)S(1)} %get-tuple-element.13.grad_own, bf16[40,32,128]{2,1,0:T(8,128)(2,1)S(1)} %get-tuple-element.14.grad_sib, f32[8,128]{1,0:T(8,128)S(1)} %get-tuple-element.15.depth), custom_call_target="tpu_custom_call" | custom-call | tf_op jit(solution)/shard_map/give_back/pallas_call | solution.py:438
  55.8 0.6 %copy.11 = f32[1,1024]{1,0:T(1,128)} copy(f32[1,1024]{1,0:T(1,128)S(1)} %get-tuple-element.20) | data formatting | bytes 8192
  56.4 0.7 %copy.12 = f32[1,32,1024]{2,1,0:T(8,128)} copy(f32[1,32,1024]{2,1,0:T(8,128)S(1)} %bitcast.6) | data formatting | bytes 262144
Async XLA Ops:
  0.6 0.7 %copy-start.4 = (f32[1,1024]{1,0:T(1,128)S(1)}, f32[1,1024]{1,0:T(1,128)}, u32[]{:S(2)}) copy-start(f32[1,1024]{1,0:T(1,128)} %cot.1) | copy-start | bytes 12292
  1.3 0.8 %copy-start.1 = (bf16[1,32,1024]{2,1,0:T(8,128)(2,1)S(1)}, bf16[1,32,1024]{2,1,0:T(8,128)(2,1)}, u32[]{:S(2)}) copy-start(bf16[1,32,1024]{2,1,0:T(8,128)(2,1)} %param.7) | copy-start | bytes 196612
  2.2 0.7 %copy-start.2 = (s32[1,4,32,8]{2,3,1,0:T(8,128)S(1)}, s32[1,4,32,8]{2,3,1,0:T(8,128)}, u32[]{:S(2)}) copy-start(s32[1,4,32,8]{2,3,1,0:T(8,128)} %param.9) | copy-start | bytes 12292
  2.9 0.7 %copy-start.5 = (s32[16,4]{0,1:T(4,128)S(1)}, s32[16,4]{0,1:T(4,128)}, u32[]{:S(2)}) copy-start(s32[16,4]{0,1:T(4,128)} %param.8) | copy-start | bytes 772
  3.6 19.7 %copy-start.3 = (bf16[3,8,32]{2,1,0:T(8,128)(2,1)S(1)}, bf16[3,8,32]{2,1,0:T(8,128)(2,1)}, u32[]{:S(2)}) copy-start(bf16[3,8,32]{2,1,0:T(8,128)(2,1)} %reg.1) | copy-start | bytes 4612
  23.3 0.7 %copy-start.6 = (f32[8]{0:T(128)S(1)}, f32[8]{0:T(128)}, u32[]{:S(2)}) copy-start(f32[8]{0:T(128)} %head.1) | copy-start | bytes 100
  24.0 1.2 %copy-start = (bf16[32,128,128]{2,1,0:T(8,128)(2,1)S(1)}, bf16[32,128,128]{2,1,0:T(8,128)(2,1)}, u32[]{:S(2)}) copy-start(bf16[32,128,128]{2,1,0:T(8,128)(2,1)} %ker.1) | copy-start | bytes 3145732

commit v2 on v1

--- a/solution.py
+++ b/solution.py
@@ -47,9 +47,32 @@
     pltpu.make_async_copy(ref, ref, semaphore).wait()
 
 
+def make_bands(taps, head, band, band_t):
+    rows = []
+    for t in range(3):
+        tap = taps[t].astype(f32)
+        rows.append(sum(head[r] * tap[r:r + 1, :] for r in range(8)))
+    row_id = lax.broadcasted_iota(i32, (8, C), 0)
+    weight = jnp.where(row_id == 0, rows[0], jnp.where(row_id == 1, rows[1], jnp.where(row_id == 2, rows[2], 0.0)))
+    w_hi = weight.astype(bf16)
+    w_lo = (weight - w_hi.astype(f32)).astype(bf16)
+    wide_lane = lax.broadcasted_iota(i32, (C, D * C), 1)
+    wide_row = lax.broadcasted_iota(i32, (C, D * C), 0)
+    spread = (wide_lane % C == wide_row).astype(f32).astype(bf16)
+    tap_of = wide_lane // C - wide_row + 1
+    bands = []
+    for part in (w_hi, w_lo):
+        wide = jnp.dot(part, spread, preferred_element_type=f32)
+        bands.append(sum(jnp.where(tap_of == t, wide[t:t + 1, :], 0.0) for t in range(3)))
+    band[...] = jnp.concatenate(bands, axis=0).astype(bf16)
+    band_t[...] = jnp.transpose(jnp.concatenate(bands + bands, axis=0)).astype(bf16)
+
+
 def exchange_kernel(
-    feats, offsets, cot, views, win, index_out, cot_out,
-    blocks, aux, aux_rx, send, recv, aux_send, aux_recv, rim_send, sib_send, sib_recv,
+    feats, offsets_hbm, cot_hbm, views_hbm, kernels, taps_hbm, head_hbm,
+    win, index_out, cot_out, diag, band, band_t,
+    blocks, offsets, cot, taps, views, head, aux, aux_rx,
+    send, recv, aux_send, aux_recv, rim_send, sib_send, sib_recv, load,
 ):
     frame, core, own, mine, tile, tiles = place()
     before, after = (tile + tiles - 1) % tiles, (tile + 1) % tiles
@@ -82,11 +105,31 @@
     signal(barrier, sibling, tile)
 
     for b in range(NB):
-        blocks[b] = feats[:, b * 128:(b + 1) * 128]
+        pltpu.make_async_copy(feats.at[:, pl.ds(b * 128, 128)], blocks.at[b], load.at[0]).start()
+    small = [
+        pltpu.make_async_copy(src, dst, load.at[n])
+        for n, (src, dst) in enumerate(
+            ((offsets_hbm, offsets), (cot_hbm, cot), (views_hbm, views), (taps_hbm, taps), (head_hbm, head)), 1
+        )
+    ]
+    half = [
+        pltpu.make_async_copy(
+            kernels.at[:, h], diag.at[:, pl.ds(h * 128, 128), pl.ds(h * 128, 128)], load.at[6 + h]
+        )
+        for h in range(2)
+    ]
+    for copy in small:
+        copy.start()
+    for copy in half:
+        copy.start()
+    win[ZERO] = jnp.zeros((C, 128), bf16)
+    small[0].wait()
+    small[1].wait()
+    for b in range(NB):
         for j in range(V):
             aux[b, :, j * D:(j + 1) * D] = offsets[j, b:b + 1, :].astype(f32)
         aux[b, :, 128:256] = cot[:, b * 128:(b + 1) * 128]
-    win[ZERO] = jnp.zeros((C, 128), bf16)
+    wait_bytes(blocks, load.at[0])
 
     pl.semaphore_wait(barrier, 7 + 4 + 1)
 
@@ -131,6 +174,10 @@
                 blocks.at[pl.ds(mine - 2 + at, count)], win.at[pl.ds(own * W + at, count)], recv.at[own]
             ).start()
 
+    corner = jnp.zeros((D // 2, 128, 128), bf16)
+    diag[:, 0:128, 128:256] = corner
+    diag[:, 128:256, 0:128] = corner
+
     def window(i):
         return win.at[pl.ds(i * W, W)]
 
@@ -146,6 +193,10 @@
         return carry
 
     lax.fori_loop(0, NF, forward, 0)
+
+    for copy in small[2:]:
+        copy.wait()
+    make_bands(taps, head, band, band_t)
 
     view_of = lax.broadcasted_iota(i32, (1, 128), 1) // D
     here = tile * NB + mine
@@ -179,54 +230,43 @@
         return carry
 
     lax.fori_loop(0, NF, settle_sibling, 0)
+    for copy in half:
+        copy.wait()
 
 
 def compute_kernel(
-    idx, head, win, ker, reg, cot, depth_out, grad_own, grad_sib, cen, vd, acc_a, acc_b, ref_acc
+    idx, win, diag, band, band_t, cot, depth_out, grad_own, grad_sib, cen, vd, acc_a, acc_b, ref_acc
 ):
     step = 2
-    rows = []
-    for t in range(3):
-        taps = reg[t].astype(f32)
-        rows.append(sum(head[r] * taps[r:r + 1, :] for r in range(8)))
-    row_id = lax.broadcasted_iota(i32, (8, C), 0)
-    weight = jnp.where(row_id == 0, rows[0], jnp.where(row_id == 1, rows[1], jnp.where(row_id == 2, rows[2], 0.0)))
-    w_hi = weight.astype(bf16)
-    w_lo = (weight - w_hi.astype(f32)).astype(bf16)
-    wide_lane = lax.broadcasted_iota(i32, (C, D * C), 1)
-    wide_row = lax.broadcasted_iota(i32, (C, D * C), 0)
-    spread = (wide_lane % C == wide_row).astype(f32).astype(bf16)
-    tap_of = wide_lane // C - wide_row + 1
-    bands = []
-    for part in (w_hi, w_lo):
-        wide = jnp.dot(part, spread, preferred_element_type=f32)
-        bands.append(sum(jnp.where(tap_of == t, wide[t:t + 1, :], 0.0) for t in range(3)))
     mean_of = 1.0 / (V + 1)
 
-    def forward(d, carry):
-        mat = ker[d]
+    def forward(p, carry):
+        mat = diag[p]
         for i0 in range(0, NF, step):
-            picks = [win[idx[i, j * D + d]] for i in range(i0, i0 + step) for j in range(V)]
+            picks = [
+                jnp.concatenate([win[idx[i, j * D + 2 * p + h]] for h in range(2)], axis=1)
+                for i in range(i0, i0 + step) for j in range(V)
+            ]
             y = jnp.dot(jnp.concatenate(picks, axis=0), mat, preferred_element_type=f32)
             for i in range(i0, i0 + step):
+              for h in range(2):
                 o = (i - i0) * V * C
-                xs = [win[i * W + 2].astype(f32)] + [y[o + j * C:o + (j + 1) * C] for j in range(V)]
+                xs = [win[i * W + 2].astype(f32)] + [y[o + j * C:o + (j + 1) * C, h * 128:(h + 1) * 128] for j in range(V)]
                 average = (((xs[0] + xs[1]) + (xs[2] + xs[3])) + xs[4]) * mean_of
                 cs = [x - average for x in xs]
                 sq = [c * c for c in cs]
                 variance = (((sq[0] + sq[1]) + (sq[2] + sq[3])) + sq[4]) * mean_of
+                d = 2 * p + h
                 vd[pl.ds(pl.multiple_of(d * C, C), C), i * 128:(i + 1) * 128] = variance.astype(bf16)
                 for j in range(V + 1):
                     cen[d, i, j] = cs[j].astype(bf16)
         return carry
 
-    lax.fori_loop(0, D, forward, 0)
-
-    band = jnp.concatenate(bands, axis=0).astype(bf16)
-    band_t = jnp.transpose(jnp.concatenate(bands + bands, axis=0)).astype(bf16)
+    lax.fori_loop(0, D // 2, forward, 0)
+
     value = (lax.broadcasted_iota(i32, (D, 128), 0).astype(f32) + 1.0) / D
     for i0 in range(0, NF, 2):
-        both = jnp.dot(band, vd[:, i0 * 128:(i0 + 2) * 128], preferred_element_type=f32)
+        both = jnp.dot(band[...], vd[:, i0 * 128:(i0 + 2) * 128], preferred_element_type=f32)
         parts = []
         for i in range(i0, i0 + 2):
             o = (i - i0) * 128
@@ -241,34 +281,35 @@
             lo = (d_pre - hi.astype(f32)).astype(bf16)
             parts.append(jnp.concatenate([hi, hi, lo, lo], axis=0))
         rhs = jnp.concatenate(parts, axis=1)
-        vd[:, i0 * 128:(i0 + 2) * 128] = jnp.dot(band_t, rhs, preferred_element_type=f32).astype(bf16)
+        vd[:, i0 * 128:(i0 + 2) * 128] = jnp.dot(band_t[...], rhs, preferred_element_type=f32).astype(bf16)
 
     acc_a[...] = jnp.zeros_like(acc_a)
     acc_b[...] = jnp.zeros_like(acc_b)
     ref_acc[...] = jnp.zeros_like(ref_acc)
 
-    def backward(d, carry):
-        mat = ker[d]
+    def backward(p, carry):
+        mat = diag[p]
         for i0 in range(0, NF, step):
             gs = []
             for i in range(i0, i0 + step):
-                dv = vd[pl.ds(pl.multiple_of(d * C, C), C), i * 128:(i + 1) * 128]
-                ref_acc[i] += (dv * cen[d, i, 0]).astype(f32)
+                dvs = [vd[pl.ds(pl.multiple_of((2 * p + h) * C, C), C), i * 128:(i + 1) * 128] for h in range(2)]
+                ref_acc[i] += (dvs[0] * cen[2 * p, i, 0]).astype(f32) + (dvs[1] * cen[2 * p + 1, i, 0]).astype(f32)
                 for j in range(V):
-                    gs.append(dv * cen[d, i, j + 1])
+                    gs.append(jnp.concatenate([dvs[h] * cen[2 * p + h, i, j + 1] for h in range(2)], axis=1))
             y = lax.dot_general(
                 jnp.concatenate(gs, axis=0), mat, (((1,), (1,)), ((), ())), preferred_element_type=f32
             )
-            for i in range(i0, i0 + step):
+            for h in range(2):
+              for i in range(i0, i0 + step):
                 acc = acc_a if i % 2 == 0 else acc_b
-                slots = [idx[i, j * D + d] for j in range(V)]
+                slots = [idx[i, j * D + 2 * p + h] for j in range(V)]
                 o = (i - i0) * V * C
-                new = [acc[slots[j]] + y[o + j * C:o + (j + 1) * C] for j in range(V)]
+                new = [acc[slots[j]] + y[o + j * C:o + (j + 1) * C, h * 128:(h + 1) * 128] for j in range(V)]
                 for j in range(V):
                     acc[slots[j]] = new[j]
         return carry
 
-    lax.fori_loop(0, D, backward, 0)
+    lax.fori_loop(0, D // 2, backward, 0)
 
     for i in range(NF):
         for k in range(W):
@@ -399,31 +440,48 @@
 def per_device(features, views, offsets, kernels, reg_weight, head_weight, depth_cot):
     vmem = pl.BlockSpec(memory_space=pltpu.VMEM)
     smem = pl.BlockSpec(memory_space=pltpu.SMEM)
+    hbm = pl.BlockSpec(memory_space=pltpu.HBM)
     dma = pltpu.SemaphoreType.DMA
     shape = jax.ShapeDtypeStruct
 
-    win, index, cot = pl.pallas_call(
+    win, index, cot, diag, band, band_t = pl.pallas_call(
         exchange_kernel,
         name="exchange",
-        out_shape=(shape((ZERO + 1, C, 128), bf16), shape((NF, 128), i32), shape((NF, 128), f32)),
-        in_specs=[vmem, vmem, vmem, smem],
-        out_specs=(vmem,) * 3,
+        out_shape=(
+            shape((ZERO + 1, C, 128), bf16), shape((NF, 128), i32), shape((NF, 128), f32),
+            shape((D // 2, 256, 256), bf16), shape((2 * D, D * C), bf16), shape((D * C, 4 * D), bf16),
+        ),
+        in_specs=[hbm] * 7,
+        out_specs=(vmem,) * 6,
         scratch_shapes=[
             pltpu.VMEM((NB, C, 128), bf16),
+            pltpu.VMEM((V, NB, D), i32),
+            pltpu.VMEM((1, NB * 128), f32),
+            pltpu.VMEM((3, 8, C), bf16),
+            pltpu.SMEM((V, 16), i32),
+            pltpu.SMEM((8,), f32),
             pltpu.VMEM((NB, 1, 256), f32),
             pltpu.VMEM((NF, 1, 256), f32),
-            dma((NB,)), dma((NF,)), dma((NB,)), dma((NF,)), dma((4,)), dma((NF,)), dma((NF,)),
+            dma((NB,)), dma((NF,)), dma((NB,)), dma((NF,)), dma((4,)), dma((NF,)), dma((NF,)), dma((8,)),
         ],
         compiler_params=pltpu.CompilerParams(
             collective_id=0, has_side_effects=True, vmem_limit_bytes=16 << 20
         ),
-    )(features.reshape(C, NB * 128), jnp.transpose(offsets[0], (0, 2, 1)), depth_cot, views.T)
+    )(
+        *(
+            pltpu.with_memory_space_constraint(x, pltpu.HBM)
+            for x in (
+                features.reshape(C, NB * 128), jnp.transpose(offsets[0], (0, 2, 1)), depth_cot, views.T,
+                kernels.reshape(D // 2, 2, 128, 128), reg_weight, head_weight,
+            )
+        )
+    )
 
     depth, grad_own, grad_sib = pl.pallas_call(
         compute_kernel,
         name="compute",
         out_shape=(shape((NF, 128), f32), shape((NF * W, C, 128), f32), shape((NF * W, C, 128), bf16)),
-        in_specs=[smem, smem, vmem, vmem, vmem, vmem],
+        in_specs=[smem] + [vmem] * 5,
         out_specs=(vmem,) * 3,
         scratch_shapes=[
             pltpu.VMEM((D, NF, V + 1, C, 128), bf16),
@@ -433,7 +491,7 @@
             pltpu.VMEM((NF, C, 128), f32),
         ],
         compiler_params=pltpu.CompilerParams(vmem_limit_bytes=40 << 20),
-    )(index, head_weight, win, kernels, reg_weight, cot)
+    )(index, win, diag, band, band_t, cot)
 
     depth_map, grad = pl.pallas_call(
         return_kernel,

time: 57.3 us -> 47.7 us (0.83)
  local copies, waits for them, and re-layouts: 6.04 us -> 1.25 us
  Pallas kernels: 50.3 us -> 45.7 us
    unnamed x16 -> x2, local copies, waits for them, and re-layouts: 6.04 us -> 1.25 us
    pallas_call x1, Pallas kernels: 19.2 us -> 14.9 us  [per_device(): pl.pallas_call(compute_kernel, name='compute', out_shape=(shape((NF, 128)...]
where the time goes in v2:
time: 47.7 us; the launch traced here: 47.6 us
  Pallas kernels  45.7 us (96%)
  local copies, waits for them, and re-layouts  1.25 us (3%)
  between operations  0.65 us (1%)
    pallas_call x1, Pallas kernels, per_device(): pl.pallas_call(exchange_kernel, name='exchange', out_shape=(shape((ZERO +...  19.4 us
    pallas_call x1, Pallas kernels, per_device(): pl.pallas_call(compute_kernel, name='compute', out_shape=(shape((NF, 128)...  14.9 us
    pallas_call x1, Pallas kernels, per_device(): pl.pallas_call(return_kernel, name='give_back', out_shape=(shape((1, NB *...  11.4 us
    unnamed x2, local copies, waits for them, and re-layouts  1.25 us

profile of v2, /device:TPU:1, one launch (start us, length us, event | category | flops | bytes accessed | tf_op | source)
XLA Modules:
  0.0 47.6 jit_solution(70825469940424236)
XLA Ops:
  0.6 19.4 %exchange.1 = (bf16[81,32,128]{2,1,0:T(8,128)(2,1)S(1)}, s32[8,128]{1,0:T(8,128)S(1)}, f32[8,128]{1,0:T(8,128)S(1)}, bf16[16,256,256]{2,1,0:T(8,128)(2,1)S(1)}, ...) custom-call(bf16[32,1024]{1,0:T(8,128)(2,1)} %bitcast.9, s32[4,8,32]{2,1,0:T(8,128)} %bitcast.10, ...), custom_call_target="tpu_custom_call" | custom-call | tf_op jit(solution)/shard_map/exchange/pallas_call | solution.py:447
  20.0 14.9 %compute.1 = (f32[8,128]{1,0:T(8,128)S(1)}, f32[40,32,128]{2,1,0:T(8,128)S(1)}, bf16[40,32,128]{2,1,0:T(8,128)(2,1)S(1)}) custom-call(s32[8,128]{1,0:T(8,128)S(1)} %get-tuple-element.13.idx, bf16[81,32,128]{2,1,0:T(8,128)(2,1)S(1)} %get-tuple-element.14.win, bf16[16,256,256]{2,1,0:T(8,128)(2,1)S(1)} %get-tuple-element.15.diag, ...), custom_call_target="tpu_custom_call" | custom-call | tf_op jit(solution)/shard_map/compute/pallas_call | solution.py:480
  34.9 11.4 %give_back.1 = (f32[1,1024]{1,0:T(1,128)S(1)}, f32[32,1024]{1,0:T(8,128)S(1)}) custom-call(f32[40,32,128]{2,1,0:T(8,128)S(1)} %get-tuple-element.19.grad_own, bf16[40,32,128]{2,1,0:T(8,128)(2,1)S(1)} %get-tuple-element.20.grad_sib, f32[8,128]{1,0:T(8,128)S(1)} %get-tuple-element.21.depth), custom_call_target="tpu_custom_call" | custom-call | tf_op jit(solution)/shard_map/give_back/pallas_call | solution.py:496
  46.3 0.6 %copy.11 = f32[1,1024]{1,0:T(1,128)} copy(f32[1,1024]{1,0:T(1,128)S(1)} %get-tuple-element.26) | data formatting | bytes 8192
  46.9 0.7 %copy.12 = f32[1,32,1024]{2,1,0:T(8,128)} copy(f32[1,32,1024]{2,1,0:T(8,128)S(1)} %bitcast.7) | data formatting | bytes 262144

commit v3 on v2

--- a/solution.py
+++ b/solution.py
@@ -86,7 +86,10 @@
 
     lax.fori_loop(1, NB, greet, 0)
 
-    @pl.when(mine < 2)
+    has_before, has_after = tile > 0, tile < tiles - 1
+    edge = ((mine < 2) & (tile == 0)) | ((mine > 5) & (tile == tiles - 1))
+
+    @pl.when((mine < 2) & has_before)
     def _():
         def greet_before(b, carry):
             signal(barrier, frame_at(b, core), before)
@@ -94,7 +97,7 @@
 
         lax.fori_loop(0, NB, greet_before, 0)
 
-    @pl.when(mine > 5)
+    @pl.when((mine > 5) & has_after)
     def _():
         def greet_after(b, carry):
             signal(barrier, frame_at(b, core), after)
@@ -123,6 +126,13 @@
     for copy in half:
         copy.start()
     win[ZERO] = jnp.zeros((C, 128), bf16)
+    for b, outside in ((0, (0, 1)), (1, (0,)), (6, (4,)), (7, (3, 4))):
+        @pl.when((mine == b) & edge)
+        def _():
+            for i in range(NF):
+                for k in outside:
+                    win[i * W + k] = jnp.zeros((C, 128), bf16)
+
     small[0].wait()
     small[1].wait()
     for b in range(NB):
@@ -131,21 +141,26 @@
         aux[b, :, 128:256] = cot[:, b * 128:(b + 1) * 128]
     wait_bytes(blocks, load.at[0])
 
-    pl.semaphore_wait(barrier, 7 + 4 + 1)
+    pl.semaphore_wait(barrier, NB + jnp.where(has_before, 2, 0) + jnp.where(has_after, 2, 0))
 
     rims = (
-        (0, 1, 4, 6, before), (0, 2, 3, 7, before),
-        (6, 2, 0, 0, after), (7, 1, 0, 1, after),
+        (0, 1, 4, 6, before, has_before), (0, 2, 3, 7, before, has_before),
+        (6, 2, 0, 0, after, has_after), (7, 1, 0, 1, after, has_after),
     )
     rim_copies = [
-        remote(
-            blocks.at[pl.ds(first, count)], win.at[pl.ds(own * W + at, count)],
-            rim_send.at[n], recv.at[own], frame_at(b, core), where,
-        )
-        for n, (first, count, at, b, where) in enumerate(rims)
+        (
+            remote(
+                blocks.at[pl.ds(first, count)], win.at[pl.ds(own * W + at, count)],
+                rim_send.at[n], recv.at[own], frame_at(b, core), where,
+            ),
+            there,
+        )
+        for n, (first, count, at, b, where, there) in enumerate(rims)
     ]
-    for copy in rim_copies:
-        copy.start()
+    for copy, there in rim_copies:
+        @pl.when(there)
+        def _():
+            copy.start()
 
     def part_copy(b, at, count):
         return remote(
@@ -188,7 +203,15 @@
 
     def forward(s, carry):
         i = (own + s) % NF
-        wait_bytes(window(i), recv.at[i])
+        @pl.when(jnp.logical_not(edge))
+        def _():
+            wait_bytes(window(i), recv.at[i])
+
+        for b, _, at, count in PARTS:
+            if count < W:
+                @pl.when((mine == b) & edge)
+                def _():
+                    wait_bytes(win.at[pl.ds(i * W + at, count)], recv.at[i])
         to_sibling(i).start()
         return carry
 
@@ -221,8 +244,10 @@
         return carry
 
     lax.fori_loop(1, NB, settle, 0)
-    for copy in rim_copies:
-        copy.wait_send()
+    for copy, there in rim_copies:
+        @pl.when(there)
+        def _():
+            copy.wait_send()
 
     def settle_sibling(i, carry):
         to_sibling(i).wait_send()
@@ -320,8 +345,8 @@
 
 
 def return_kernel(
-    grad_own, grad_sib, depth, depth_out, grad_out,
-    sib_rx, out, depths, depth_rx, rx, send, recv, rim_send, depth_send, depth_recv, sib_send, sib_recv,
+    grad_own, grad_sib, depth, depth_rx, rx,
+    sib_rx, out, depths, send, recv, rim_send, depth_send, depth_recv, sib_send, sib_recv,
 ):
     frame, core, own, mine, tile, tiles = place()
     before, after = (tile + tiles - 1) % tiles, (tile + 1) % tiles
@@ -335,12 +360,33 @@
         return carry
 
     lax.fori_loop(1, NB, greet, 0)
-    for b, where in ((6, before), (7, before), (0, after), (1, after)):
-        signal(barrier, frame_at(b, core), where)
+    has_before, has_after = tile > 0, tile < tiles - 1
+
+    @pl.when(has_before)
+    def _():
+        for b in (6, 7):
+            signal(barrier, frame_at(b, core), before)
+
+    @pl.when(has_after)
+    def _():
+        for b in (0, 1):
+            signal(barrier, frame_at(b, core), after)
+
+    outer = [
+        (slot, first - slot + 4, last - first + 1, has_before if slot < 2 else has_after)
+        for slot in (0, 1, NB + 2, NB + 3)
+        for first, last in [(max(slot - 4, 0), min(slot, NB - 1))]
+    ]
+    for slot, at, count, there in outer:
+        @pl.when(jnp.logical_not(there))
+        def _():
+            for k in range(at, at + count):
+                rx[slot, k] = jnp.zeros((C, 128), bf16)
+
     for i in range(NF):
         depths[i] = depth[i:i + 1, :]
 
-    pl.semaphore_wait(barrier, jnp.where((mine < 2) | (mine > 5), 2 * NB, NB))
+    pl.semaphore_wait(barrier, jnp.where(((mine < 2) & has_before) | ((mine > 5) & has_after), 2 * NB, NB))
 
     def window(ref, i):
         return ref.at[pl.ds(i * W, W)]
@@ -373,15 +419,18 @@
             depths.at[i], depth_rx.at[mine], depth_send.at[i], depth_recv.at[mine], 2 * i + core, tile
         )
 
-    rims = ((0, 0, 2, 10, before), (1, 0, 1, 11, before), (6, 4, 1, 0, after), (7, 3, 2, 1, after))
+    rims = (
+        (0, 0, 2, 10, before, has_before), (1, 0, 1, 11, before, has_before),
+        (6, 4, 1, 0, after, has_after), (7, 3, 2, 1, after, has_after),
+    )
 
     def add_and_send(s, carry):
         i = (own + s) % NF
         wait_bytes(window(sib_rx, i), sib_recv.at[i])
         for k in range(W):
             out[i * W + k] = (grad_own[i * W + k] + sib_rx[i * W + k].astype(f32)).astype(bf16)
-        for b, at, count, slot, where in rims:
-            @pl.when(mine == b)
+        for b, at, count, slot, where, there in rims:
+            @pl.when((mine == b) & there)
             def _():
                 rim_copy(i, at, count, slot, where).start()
 
@@ -406,21 +455,19 @@
 
     for b in range(NB):
         wait_bytes(depth_rx.at[b], depth_recv.at[b])
-        depth_out[:, b * 128:(b + 1) * 128] = depth_rx[b]
-    for slot in range(NB + 4):
+    for slot in range(2, NB + 2):
         first, last = max(slot - 4, 0), min(slot, NB - 1)
         wait_bytes(rx.at[slot, pl.ds(first - slot + 4, last - first + 1)], recv.at[slot])
-    for b in range(NB):
-        total = rx[b, 4].astype(f32)
-        for k in range(1, W):
-            total += rx[b + k, 4 - k].astype(f32)
-        grad_out[:, b * 128:(b + 1) * 128] = total
+    for slot, at, count, there in outer:
+        @pl.when(there)
+        def _():
+            wait_bytes(rx.at[slot, pl.ds(at, count)], recv.at[slot])
 
     def settle(s, carry):
         i = (own + s) % NF
         to_sibling(i).wait_send()
-        for b, at, count, slot, where in rims:
-            @pl.when(mine == b)
+        for b, at, count, slot, where, there in rims:
+            @pl.when((mine == b) & there)
             def _():
                 rim_copy(i, at, count, slot, where).wait_send()
 
@@ -435,6 +482,15 @@
         return carry
 
     lax.fori_loop(1, NF + 1, settle, 0)
+
+
+def sum_kernel(depth_rx, rx, depth_out, grad_out):
+    for b in range(NB):
+        depth_out[:, b * 128:(b + 1) * 128] = depth_rx[b]
+        total = rx[b, 4].astype(f32)
+        for k in range(1, W):
+            total += rx[b + k, 4 - k].astype(f32)
+        grad_out[:, b * 128:(b + 1) * 128] = total
 
 
 def per_device(features, views, offsets, kernels, reg_weight, head_weight, depth_cot):
@@ -493,24 +549,31 @@
         compiler_params=pltpu.CompilerParams(vmem_limit_bytes=40 << 20),
     )(index, win, diag, band, band_t, cot)
 
-    depth_map, grad = pl.pallas_call(
+    depth_rx, rx = pl.pallas_call(
         return_kernel,
         name="give_back",
-        out_shape=(shape((1, NB * 128), f32), shape((C, NB * 128), f32)),
+        out_shape=(shape((NB, 1, 128), f32), shape((NB + 4, W, C, 128), bf16)),
         in_specs=[vmem] * 3,
         out_specs=(vmem,) * 2,
         scratch_shapes=[
             pltpu.VMEM((NF * W, C, 128), bf16),
             pltpu.VMEM((NF * W, C, 128), bf16),
             pltpu.VMEM((NF, 1, 128), f32),
-            pltpu.VMEM((NB, 1, 128), f32),
-            pltpu.VMEM((NB + 4, W, C, 128), bf16),
             dma((NF,)), dma((NB + 4,)), dma((NF,)), dma((NF,)), dma((NB,)), dma((NF,)), dma((NF,)),
         ],
         compiler_params=pltpu.CompilerParams(
             collective_id=1, has_side_effects=True, vmem_limit_bytes=16 << 20
         ),
     )(grad_own, grad_sib, depth)
+
+    depth_map, grad = pl.pallas_call(
+        sum_kernel,
+        name="total",
+        out_shape=(shape((1, NB * 128), f32), shape((C, NB * 128), f32)),
+        in_specs=[vmem] * 2,
+        out_specs=(vmem,) * 2,
+        compiler_params=pltpu.CompilerParams(vmem_limit_bytes=8 << 20),
+    )(depth_rx, rx)
     return depth_map, grad.reshape(1, C, NB * 128)
 
 

time: 47.7 us -> 42.2 us (0.88)
  the two profiles are of different devices: /device:TPU:1 before, /device:TPU:100 now
where the time goes in v3:
time: 42.2 us; the launch traced here: 42.1 us
  Pallas kernels  41.5 us (98%)
  between operations  0.65 us (2%)
    pallas_call x1, Pallas kernels, per_device(): pl.pallas_call(compute_kernel, name='compute', out_shape=(shape((NF, 128)...  14.9 us
    pallas_call x1, Pallas kernels, per_device(): pl.pallas_call(return_kernel, name='give_back', out_shape=(shape((NB, 1,...  13.5 us
    pallas_call x1, Pallas kernels, per_device(): pl.pallas_call(exchange_kernel, name='exchange', out_shape=(shape((ZERO +...  12.4 us

profile of v3, /device:TPU:100, one launch (start us, length us, event | category | flops | bytes accessed | tf_op | source)
XLA Modules:
  0.0 42.1 jit_solution(14632855922793196889)
XLA Ops:
  0.6 12.4 %exchange.1 = (bf16[81,32,128]{2,1,0:T(8,128)(2,1)S(1)}, s32[8,128]{1,0:T(8,128)S(1)}, f32[8,128]{1,0:T(8,128)S(1)}, bf16[16,256,256]{2,1,0:T(8,128)(2,1)S(1)}, ...) custom-call(bf16[32,1024]{1,0:T(8,128)(2,1)} %bitcast.8, s32[4,8,32]{2,1,0:T(8,128)} %bitcast.9, ...), custom_call_target="tpu_custom_call" | custom-call | tf_op jit(solution)/shard_map/exchange/pallas_call | solution.py:503
  13.1 14.9 %compute.1 = (f32[8,128]{1,0:T(8,128)S(1)}, f32[40,32,128]{2,1,0:T(8,128)S(1)}, bf16[40,32,128]{2,1,0:T(8,128)(2,1)S(1)}) custom-call(s32[8,128]{1,0:T(8,128)S(1)} %get-tuple-element.15.idx, bf16[81,32,128]{2,1,0:T(8,128)(2,1)S(1)} %get-tuple-element.16.win, bf16[16,256,256]{2,1,0:T(8,128)(2,1)S(1)} %get-tuple-element.17.diag, ...), custom_call_target="tpu_custom_call" | custom-call | tf_op jit(solution)/shard_map/compute/pallas_call | solution.py:536
  27.9 13.5 %give_back.1 = (f32[8,1,128]{2,1,0:T(1,128)S(1)}, bf16[12,5,32,128]{3,2,1,0:T(8,128)(2,1)S(1)}) custom-call(f32[40,32,128]{2,1,0:T(8,128)S(1)} %get-tuple-element.21.grad_own, bf16[40,32,128]{2,1,0:T(8,128)(2,1)S(1)} %get-tuple-element.22.grad_sib, f32[8,128]{1,0:T(8,128)S(1)} %get-tuple-element.23.depth), custom_call_target="tpu_custom_call" | custom-call | tf_op jit(solution)/shard_map/give_back/pallas_call | solution.py:552
  41.4 0.7 %total.1 = (f32[1,1024]{1,0:T(1,128)}, f32[32,1024]{1,0:T(8,128)}) custom-call(f32[8,1,128]{2,1,0:T(1,128)S(1)} %get-tuple-element.24.depth_rx, bf16[12,5,32,128]{3,2,1,0:T(8,128)(2,1)S(1)} %get-tuple-element.25.rx), custom_call_target="tpu_custom_call" | custom-call | tf_op jit(solution)/shard_map/total/pallas_call | solution.py:569

commit v4 on v3

--- a/solution.py
+++ b/solution.py
@@ -259,13 +259,11 @@
         copy.wait()
 
 
-def compute_kernel(
-    idx, win, diag, band, band_t, cot, depth_out, grad_own, grad_sib, cen, vd, acc_a, acc_b, ref_acc
-):
+def compute_kernel(idx, win, diag, band, band_t, cot, depth_out, acc, ref_acc, cen, vd):
     step = 2
     mean_of = 1.0 / (V + 1)
 
-    def forward(p, carry):
+    for p in range(D // 2):
         mat = diag[p]
         for i0 in range(0, NF, step):
             picks = [
@@ -274,20 +272,17 @@
             ]
             y = jnp.dot(jnp.concatenate(picks, axis=0), mat, preferred_element_type=f32)
             for i in range(i0, i0 + step):
-              for h in range(2):
-                o = (i - i0) * V * C
-                xs = [win[i * W + 2].astype(f32)] + [y[o + j * C:o + (j + 1) * C, h * 128:(h + 1) * 128] for j in range(V)]
-                average = (((xs[0] + xs[1]) + (xs[2] + xs[3])) + xs[4]) * mean_of
-                cs = [x - average for x in xs]
-                sq = [c * c for c in cs]
-                variance = (((sq[0] + sq[1]) + (sq[2] + sq[3])) + sq[4]) * mean_of
-                d = 2 * p + h
-                vd[pl.ds(pl.multiple_of(d * C, C), C), i * 128:(i + 1) * 128] = variance.astype(bf16)
-                for j in range(V + 1):
-                    cen[d, i, j] = cs[j].astype(bf16)
-        return carry
-
-    lax.fori_loop(0, D // 2, forward, 0)
+                for h in range(2):
+                    o, d = (i - i0) * V * C, 2 * p + h
+                    xs = [win[i * W + 2].astype(f32)]
+                    xs += [y[o + j * C:o + (j + 1) * C, h * 128:(h + 1) * 128] for j in range(V)]
+                    average = (((xs[0] + xs[1]) + (xs[2] + xs[3])) + xs[4]) * mean_of
+                    cs = [x - average for x in xs]
+                    sq = [c * c for c in cs]
+                    variance = (((sq[0] + sq[1]) + (sq[2] + sq[3])) + sq[4]) * mean_of
+                    vd[d * C:(d + 1) * C, i * 128:(i + 1) * 128] = variance.astype(bf16)
+                    for j in range(V + 1):
+                        cen[d, i, j] = cs[j].astype(bf16)
 
     value = (lax.broadcasted_iota(i32, (D, 128), 0).astype(f32) + 1.0) / D
     for i0 in range(0, NF, 2):
@@ -299,7 +294,7 @@
             w = jnp.exp(4.0 * th)
             total = jnp.sum(w, axis=0, keepdims=True)
             depth = jnp.sum(w * value, axis=0, keepdims=True) / total
-            depth_out[i:i + 1, :] = depth
+            depth_out[i] = depth
             scale = cot[i:i + 1, :] / total * (4.0 * 2.0 / (V + 1))
             d_pre = (w * (value - depth)) * scale * (1.0 - th * th)
             hi = d_pre.astype(bf16)
@@ -308,16 +303,15 @@
         rhs = jnp.concatenate(parts, axis=1)
         vd[:, i0 * 128:(i0 + 2) * 128] = jnp.dot(band_t[...], rhs, preferred_element_type=f32).astype(bf16)
 
-    acc_a[...] = jnp.zeros_like(acc_a)
-    acc_b[...] = jnp.zeros_like(acc_b)
+    acc[...] = jnp.zeros_like(acc)
     ref_acc[...] = jnp.zeros_like(ref_acc)
 
-    def backward(p, carry):
+    for p in range(D // 2):
         mat = diag[p]
         for i0 in range(0, NF, step):
             gs = []
             for i in range(i0, i0 + step):
-                dvs = [vd[pl.ds(pl.multiple_of((2 * p + h) * C, C), C), i * 128:(i + 1) * 128] for h in range(2)]
+                dvs = [vd[(2 * p + h) * C:(2 * p + h + 1) * C, i * 128:(i + 1) * 128] for h in range(2)]
                 ref_acc[i] += (dvs[0] * cen[2 * p, i, 0]).astype(f32) + (dvs[1] * cen[2 * p + 1, i, 0]).astype(f32)
                 for j in range(V):
                     gs.append(jnp.concatenate([dvs[h] * cen[2 * p + h, i, j + 1] for h in range(2)], axis=1))
@@ -325,28 +319,17 @@
                 jnp.concatenate(gs, axis=0), mat, (((1,), (1,)), ((), ())), preferred_element_type=f32
             )
             for h in range(2):
-              for i in range(i0, i0 + step):
-                acc = acc_a if i % 2 == 0 else acc_b
-                slots = [idx[i, j * D + 2 * p + h] for j in range(V)]
-                o = (i - i0) * V * C
-                new = [acc[slots[j]] + y[o + j * C:o + (j + 1) * C, h * 128:(h + 1) * 128] for j in range(V)]
-                for j in range(V):
-                    acc[slots[j]] = new[j]
-        return carry
-
-    lax.fori_loop(0, D // 2, backward, 0)
-
-    for i in range(NF):
-        for k in range(W):
-            s = i * W + k
-            total = acc_a[s] + acc_b[s]
-            grad_own[s] = total + ref_acc[i] if k == 2 else total
-            grad_sib[s] = (acc_a[NF * W + s] + acc_b[NF * W + s]).astype(bf16)
+                for i in range(i0, i0 + step):
+                    slots = [idx[i, j * D + 2 * p + h] for j in range(V)]
+                    o = (i - i0) * V * C
+                    new = [acc[slots[j]] + y[o + j * C:o + (j + 1) * C, h * 128:(h + 1) * 128] for j in range(V)]
+                    for j in range(V):
+                        acc[slots[j]] = new[j]
 
 
 def return_kernel(
-    grad_own, grad_sib, depth, depth_rx, rx,
-    sib_rx, out, depths, send, recv, rim_send, depth_send, depth_recv, sib_send, sib_recv,
+    acc, ref_acc, depths, depth_rx, rx,
+    grad_sib, sib_rx, out, send, recv, rim_send, depth_send, depth_recv, sib_send, sib_recv,
 ):
     frame, core, own, mine, tile, tiles = place()
     before, after = (tile + tiles - 1) % tiles, (tile + 1) % tiles
@@ -383,8 +366,8 @@
             for k in range(at, at + count):
                 rx[slot, k] = jnp.zeros((C, 128), bf16)
 
-    for i in range(NF):
-        depths[i] = depth[i:i + 1, :]
+    for s in range(NF * W):
+        grad_sib[s] = acc[NF * W + s].astype(bf16)
 
     pl.semaphore_wait(barrier, jnp.where(((mine < 2) & has_before) | ((mine > 5) & has_after), 2 * NB, NB))
 
@@ -428,7 +411,8 @@
         i = (own + s) % NF
         wait_bytes(window(sib_rx, i), sib_recv.at[i])
         for k in range(W):
-            out[i * W + k] = (grad_own[i * W + k] + sib_rx[i * W + k].astype(f32)).astype(bf16)
+            total = acc[i * W + k] + sib_rx[i * W + k].astype(f32)
+            out[i * W + k] = (total + ref_acc[i] if k == 2 else total).astype(bf16)
         for b, at, count, slot, where, there in rims:
             @pl.when((mine == b) & there)
             def _():
@@ -533,18 +517,15 @@
         )
     )
 
-    depth, grad_own, grad_sib = pl.pallas_call(
+    depths, acc, ref_acc = pl.pallas_call(
         compute_kernel,
         name="compute",
-        out_shape=(shape((NF, 128), f32), shape((NF * W, C, 128), f32), shape((NF * W, C, 128), bf16)),
+        out_shape=(shape((NF, 1, 128), f32), shape((ZERO + 1, C, 128), f32), shape((NF, C, 128), f32)),
         in_specs=[smem] + [vmem] * 5,
         out_specs=(vmem,) * 3,
         scratch_shapes=[
             pltpu.VMEM((D, NF, V + 1, C, 128), bf16),
             pltpu.VMEM((D * C, NF * 128), bf16),
-            pltpu.VMEM((ZERO + 1, C, 128), f32),
-            pltpu.VMEM((ZERO + 1, C, 128), f32),
-            pltpu.VMEM((NF, C, 128), f32),
         ],
         compiler_params=pltpu.CompilerParams(vmem_limit_bytes=40 << 20),
     )(index, win, diag, band, band_t, cot)
@@ -558,13 +539,13 @@
         scratch_shapes=[
             pltpu.VMEM((NF * W, C, 128), bf16),
             pltpu.VMEM((NF * W, C, 128), bf16),
-            pltpu.VMEM((NF, 1, 128), f32),
+            pltpu.VMEM((NF * W, C, 128), bf16),
             dma((NF,)), dma((NB + 4,)), dma((NF,)), dma((NF,)), dma((NB,)), dma((NF,)), dma((NF,)),
         ],
         compiler_params=pltpu.CompilerParams(
             collective_id=1, has_side_effects=True, vmem_limit_bytes=16 << 20
         ),
-    )(grad_own, grad_sib, depth)
+    )(acc, ref_acc, depths)
 
     depth_map, grad = pl.pallas_call(
         sum_kernel,

time: 42.2 us -> 37.8 us (0.90)
  Pallas kernels: 41.5 us -> 37.1 us
    pallas_call x1, Pallas kernels: 14.9 us -> 10.5 us  [per_device(): pl.pallas_call(compute_kernel, name='compute', out_shape=(shape((NF, 1, 1...]
where the time goes in v4:
time: 37.8 us; the launch traced here: 37.7 us
  Pallas kernels  37.1 us (98%)
  between operations  0.66 us (2%)
    pallas_call x1, Pallas kernels, per_device(): pl.pallas_call(return_kernel, name='give_back', out_shape=(shape((NB, 1,...  13.5 us
    pallas_call x1, Pallas kernels, per_device(): pl.pallas_call(exchange_kernel, name='exchange', out_shape=(shape((ZERO +...  12.4 us
    pallas_call x1, Pallas kernels, per_device(): pl.pallas_call(compute_kernel, name='compute', out_shape=(shape((NF, 1, 1...  10.5 us

profile of v4, /device:TPU:100, one launch (start us, length us, event | category | flops | bytes accessed | tf_op | source)
XLA Modules:
  0.0 37.7 jit_solution(12053933470974595532)
XLA Ops:
  0.6 12.4 %exchange.1 = (bf16[81,32,128]{2,1,0:T(8,128)(2,1)S(1)}, s32[8,128]{1,0:T(8,128)S(1)}, f32[8,128]{1,0:T(8,128)S(1)}, bf16[16,256,256]{2,1,0:T(8,128)(2,1)S(1)}, ...) custom-call(bf16[32,1024]{1,0:T(8,128)(2,1)} %bitcast.8, s32[4,8,32]{2,1,0:T(8,128)} %bitcast.9, ...), custom_call_target="tpu_custom_call" | custom-call | tf_op jit(solution)/shard_map/exchange/pallas_call | solution.py:487
  13.1 10.5 %compute.1 = (f32[8,1,128]{2,1,0:T(1,128)S(1)}, f32[81,32,128]{2,1,0:T(8,128)S(1)}, f32[8,32,128]{2,1,0:T(8,128)S(1)}) custom-call(s32[8,128]{1,0:T(8,128)S(1)} %get-tuple-element.15.idx, bf16[81,32,128]{2,1,0:T(8,128)(2,1)S(1)} %get-tuple-element.16.win, bf16[16,256,256]{2,1,0:T(8,128)(2,1)S(1)} %get-tuple-element.17.diag, ...), custom_call_target="tpu_custom_call" | custom-call | tf_op jit(solution)/shard_map/compute/pallas_call | solution.py:520
  23.6 13.5 %give_back.1 = (f32[8,1,128]{2,1,0:T(1,128)S(1)}, bf16[12,5,32,128]{3,2,1,0:T(8,128)(2,1)S(1)}) custom-call(f32[81,32,128]{2,1,0:T(8,128)S(1)} %get-tuple-element.21.acc, f32[8,32,128]{2,1,0:T(8,128)S(1)} %get-tuple-element.22.ref_acc, f32[8,1,128]{2,1,0:T(1,128)S(1)} %get-tuple-element.23.depths), custom_call_target="tpu_custom_call" | custom-call | tf_op jit(solution)/shard_map/give_back/pallas_call | solution.py:533
  37.0 0.7 %total.1 = (f32[1,1024]{1,0:T(1,128)}, f32[32,1024]{1,0:T(8,128)}) custom-call(f32[8,1,128]{2,1,0:T(1,128)S(1)} %get-tuple-element.24.depth_rx, bf16[12,5,32,128]{3,2,1,0:T(8,128)(2,1)S(1)} %get-tuple-element.25.rx), custom_call_target="tpu_custom_call" | custom-call | tf_op jit(solution)/shard_map/total/pallas_call | solution.py:550

commit v5 on v4

--- a/solution.py
+++ b/solution.py
@@ -47,7 +47,7 @@
     pltpu.make_async_copy(ref, ref, semaphore).wait()
 
 
-def make_bands(taps, head, band, band_t):
+def make_bands(taps, head, band, columns):
     rows = []
     for t in range(3):
         tap = taps[t].astype(f32)
@@ -65,12 +65,14 @@
         wide = jnp.dot(part, spread, preferred_element_type=f32)
         bands.append(sum(jnp.where(tap_of == t, wide[t:t + 1, :], 0.0) for t in range(3)))
     band[...] = jnp.concatenate(bands, axis=0).astype(bf16)
-    band_t[...] = jnp.transpose(jnp.concatenate(bands + bands, axis=0)).astype(bf16)
+    upright = jnp.transpose(jnp.concatenate([weight, jnp.zeros((8, 128 - C), f32)], axis=1))
+    for t in range(3):
+        columns[t] = jnp.broadcast_to(upright[:C, t:t + 1], (C, 128))
 
 
 def exchange_kernel(
     feats, offsets_hbm, cot_hbm, views_hbm, kernels, taps_hbm, head_hbm,
-    win, index_out, cot_out, diag, band, band_t,
+    win, index_out, cot_out, diag, band, columns,
     blocks, offsets, cot, taps, views, head, aux, aux_rx,
     send, recv, aux_send, aux_recv, rim_send, sib_send, sib_recv, load,
 ):
@@ -171,8 +173,8 @@
     def aux_copy(b):
         return remote(aux.at[b], aux_rx.at[own], aux_send.at[b], aux_recv.at[own], frame_at(b, core), tile)
 
-    def start(s, carry):
-        b = (mine + s) % NB
+    def start(n, carry):
+        b = (mine + jnp.where(n % 2 == 1, 4 - (n + 1) // 2, 4 + n // 2)) % NB
         aux_copy(b).start()
         for least, most, at, count in PARTS:
             @pl.when((b >= least) & (b <= most))
@@ -180,7 +182,7 @@
                 part_copy(b, at, count).start()
         return carry
 
-    lax.fori_loop(1, NB, start, 0)
+    lax.fori_loop(0, NB - 1, start, 0)
     pltpu.make_async_copy(aux.at[mine], aux_rx.at[own], aux_recv.at[own]).start()
     for least, most, at, count in PARTS:
         @pl.when((mine >= least) & (mine <= most))
@@ -192,6 +194,9 @@
     corner = jnp.zeros((D // 2, 128, 128), bf16)
     diag[:, 0:128, 128:256] = corner
     diag[:, 128:256, 0:128] = corner
+    for copy in small[2:]:
+        copy.wait()
+    make_bands(taps, head, band, columns)
 
     def window(i):
         return win.at[pl.ds(i * W, W)]
@@ -216,10 +221,6 @@
         return carry
 
     lax.fori_loop(0, NF, forward, 0)
-
-    for copy in small[2:]:
-        copy.wait()
-    make_bands(taps, head, band, band_t)
 
     view_of = lax.broadcasted_iota(i32, (1, 128), 1) // D
     here = tile * NB + mine
@@ -259,7 +260,7 @@
         copy.wait()
 
 
-def compute_kernel(idx, win, diag, band, band_t, cot, depth_out, acc, ref_acc, cen, vd):
+def compute_kernel(idx, win, diag, band, columns, cot, depth_out, acc, ref_acc, cen, vd, d_pre):
     step = 2
     mean_of = 1.0 / (V + 1)
 
@@ -287,7 +288,6 @@
     value = (lax.broadcasted_iota(i32, (D, 128), 0).astype(f32) + 1.0) / D
     for i0 in range(0, NF, 2):
         both = jnp.dot(band[...], vd[:, i0 * 128:(i0 + 2) * 128], preferred_element_type=f32)
-        parts = []
         for i in range(i0, i0 + 2):
             o = (i - i0) * 128
             th = jnp.tanh(both[:D, o:o + 128] + both[D:, o:o + 128])
@@ -296,12 +296,7 @@
             depth = jnp.sum(w * value, axis=0, keepdims=True) / total
             depth_out[i] = depth
             scale = cot[i:i + 1, :] / total * (4.0 * 2.0 / (V + 1))
-            d_pre = (w * (value - depth)) * scale * (1.0 - th * th)
-            hi = d_pre.astype(bf16)
-            lo = (d_pre - hi.astype(f32)).astype(bf16)
-            parts.append(jnp.concatenate([hi, hi, lo, lo], axis=0))
-        rhs = jnp.concatenate(parts, axis=1)
-        vd[:, i0 * 128:(i0 + 2) * 128] = jnp.dot(band_t[...], rhs, preferred_element_type=f32).astype(bf16)
+            d_pre[i] = (w * (value - depth)) * scale * (1.0 - th * th)
 
     acc[...] = jnp.zeros_like(acc)
     ref_acc[...] = jnp.zeros_like(ref_acc)
@@ -311,7 +306,10 @@
         for i0 in range(0, NF, step):
             gs = []
             for i in range(i0, i0 + step):
-                dvs = [vd[(2 * p + h) * C:(2 * p + h + 1) * C, i * 128:(i + 1) * 128] for h in range(2)]
+                dvs = []
+                for d in (2 * p, 2 * p + 1):
+                    terms = [columns[t] * d_pre[i, d - t + 1:d - t + 2, :] for t in range(3) if 0 <= d - t + 1 < D]
+                    dvs.append(sum(terms[1:], terms[0]).astype(bf16))
                 ref_acc[i] += (dvs[0] * cen[2 * p, i, 0]).astype(f32) + (dvs[1] * cen[2 * p + 1, i, 0]).astype(f32)
                 for j in range(V):
                     gs.append(jnp.concatenate([dvs[h] * cen[2 * p + h, i, j + 1] for h in range(2)], axis=1))
@@ -379,11 +377,15 @@
             window(grad_sib, i), window(sib_rx, i), sib_send.at[i], sib_recv.at[i], sibling, tile
         )
 
-    def start_sibling(s, carry):
-        to_sibling((own + s) % NF).start()
-        return carry
-
-    lax.fori_loop(1, NF + 1, start_sibling, 0)
+    def owner(n):
+        across, along = 1 - n % 2, jnp.where(n < 2, 2, jnp.where(n < 4, 1, jnp.where(n < 6, 3, 0)))
+        return ((own // 4 + across) % 2) * 4 + (own % 4 + along) % 4
+
+    def start_sibling(n, carry):
+        to_sibling(owner(n)).start()
+        return carry
+
+    lax.fori_loop(0, NF, start_sibling, 0)
 
     def part_copy(i, at, count):
         return remote(
@@ -407,8 +409,19 @@
         (6, 4, 1, 0, after, has_after), (7, 3, 2, 1, after, has_after),
     )
 
-    def add_and_send(s, carry):
-        i = (own + s) % NF
+    def send_parts(i):
+        @pl.when(i != own)
+        def _():
+            depth_copy(i).start()
+            for least, most, at, count in PARTS:
+                @pl.when((mine >= least) & (mine <= most))
+                def _():
+                    part_copy(i, at, count).start()
+
+    at_edge = (mine < 2) | (mine > 5)
+
+    def add_and_send(n, carry):
+        i = owner(n)
         wait_bytes(window(sib_rx, i), sib_recv.at[i])
         for k in range(W):
             total = acc[i * W + k] + sib_rx[i * W + k].astype(f32)
@@ -418,17 +431,22 @@
             def _():
                 rim_copy(i, at, count, slot, where).start()
 
-        @pl.when(i != own)
-        def _():
-            depth_copy(i).start()
-            for least, most, at, count in PARTS:
-                @pl.when((mine >= least) & (mine <= most))
-                def _():
-                    part_copy(i, at, count).start()
-
-        return carry
-
-    lax.fori_loop(1, NF + 1, add_and_send, 0)
+        @pl.when(jnp.logical_not(at_edge))
+        def _():
+            send_parts(i)
+
+        return carry
+
+    lax.fori_loop(0, NF, add_and_send, 0)
+
+    @pl.when(at_edge)
+    def _():
+        def send_later(n, carry):
+            send_parts(owner(n))
+            return carry
+
+        lax.fori_loop(0, NF, send_later, 0)
+
     pltpu.make_async_copy(depths.at[own], depth_rx.at[mine], depth_recv.at[mine]).start()
     for least, most, at, count in PARTS:
         @pl.when((mine >= least) & (mine <= most))
@@ -484,12 +502,12 @@
     dma = pltpu.SemaphoreType.DMA
     shape = jax.ShapeDtypeStruct
 
-    win, index, cot, diag, band, band_t = pl.pallas_call(
+    win, index, cot, diag, band, columns = pl.pallas_call(
         exchange_kernel,
         name="exchange",
         out_shape=(
             shape((ZERO + 1, C, 128), bf16), shape((NF, 128), i32), shape((NF, 128), f32),
-            shape((D // 2, 256, 256), bf16), shape((2 * D, D * C), bf16), shape((D * C, 4 * D), bf16),
+            shape((D // 2, 256, 256), bf16), shape((2 * D, D * C), bf16), shape((3, C, 128), f32),
         ),
         in_specs=[hbm] * 7,
         out_specs=(vmem,) * 6,
@@ -526,9 +544,10 @@
         scratch_shapes=[
             pltpu.VMEM((D, NF, V + 1, C, 128), bf16),
             pltpu.VMEM((D * C, NF * 128), bf16),
+            pltpu.VMEM((NF, D, 128), f32),
         ],
         compiler_params=pltpu.CompilerParams(vmem_limit_bytes=40 << 20),
-    )(index, win, diag, band, band_t, cot)
+    )(index, win, diag, band, columns, cot)
 
     depth_rx, rx = pl.pallas_call(
         return_kernel,

time: 37.8 us -> 37.1 us (0.981)
  Pallas kernels: 37.1 us -> 36.4 us
    pallas_call x1, Pallas kernels: 10.5 us -> 9.87 us  [per_device(): pl.pallas_call(compute_kernel, name='compute', out_shape=(shape((NF, 1, 1...]
where the time goes in v5:
time: 37.1 us; the launch traced here: 37 us
  Pallas kernels  36.4 us (98%)
  between operations  0.65 us (2%)
    pallas_call x1, Pallas kernels, per_device(): pl.pallas_call(return_kernel, name='give_back', out_shape=(shape((NB, 1,...  13.1 us
    pallas_call x1, Pallas kernels, per_device(): pl.pallas_call(exchange_kernel, name='exchange', out_shape=(shape((ZERO +...  12.7 us
    pallas_call x1, Pallas kernels, per_device(): pl.pallas_call(compute_kernel, name='compute', out_shape=(shape((NF, 1, 1...  9.87 us

profile of v5, /device:TPU:100, one launch (start us, length us, event | category | flops | bytes accessed | tf_op | source)
XLA Modules:
  0.0 37.0 jit_solution(6197809013161763956)
XLA Ops:
  0.6 12.7 %exchange.1 = (bf16[81,32,128]{2,1,0:T(8,128)(2,1)S(1)}, s32[8,128]{1,0:T(8,128)S(1)}, f32[8,128]{1,0:T(8,128)S(1)}, bf16[16,256,256]{2,1,0:T(8,128)(2,1)S(1)}, ...) custom-call(bf16[32,1024]{1,0:T(8,128)(2,1)} %bitcast.8, s32[4,8,32]{2,1,0:T(8,128)} %bitcast.9, ...), custom_call_target="tpu_custom_call" | custom-call | tf_op jit(solution)/shard_map/exchange/pallas_call | solution.py:505
  13.3 9.9 %compute.1 = (f32[8,1,128]{2,1,0:T(1,128)S(1)}, f32[81,32,128]{2,1,0:T(8,128)S(1)}, f32[8,32,128]{2,1,0:T(8,128)S(1)}) custom-call(s32[8,128]{1,0:T(8,128)S(1)} %get-tuple-element.15.idx, bf16[81,32,128]{2,1,0:T(8,128)(2,1)S(1)} %get-tuple-element.16.win, bf16[16,256,256]{2,1,0:T(8,128)(2,1)S(1)} %get-tuple-element.17.diag, ...), custom_call_target="tpu_custom_call" | custom-call | tf_op jit(solution)/shard_map/compute/pallas_call | solution.py:538
  23.2 13.1 %give_back.1 = (f32[8,1,128]{2,1,0:T(1,128)S(1)}, bf16[12,5,32,128]{3,2,1,0:T(8,128)(2,1)S(1)}) custom-call(f32[81,32,128]{2,1,0:T(8,128)S(1)} %get-tuple-element.21.acc, f32[8,32,128]{2,1,0:T(8,128)S(1)} %get-tuple-element.22.ref_acc, f32[8,1,128]{2,1,0:T(1,128)S(1)} %get-tuple-element.23.depths), custom_call_target="tpu_custom_call" | custom-call | tf_op jit(solution)/shard_map/give_back/pallas_call | solution.py:552
  36.3 0.7 %total.1 = (f32[1,1024]{1,0:T(1,128)}, f32[32,1024]{1,0:T(8,128)}) custom-call(f32[8,1,128]{2,1,0:T(1,128)S(1)} %get-tuple-element.24.depth_rx, bf16[12,5,32,128]{3,2,1,0:T(8,128)(2,1)S(1)} %get-tuple-element.25.rx), custom_call_target="tpu_custom_call" | custom-call | tf_op jit(solution)/shard_map/total/pallas_call | solution.py:569

commit v6 on v5

--- a/solution.py
+++ b/solution.py
@@ -82,12 +82,6 @@
 
     barrier = pltpu.get_barrier_semaphore()
 
-    def greet(s, carry):
-        signal(barrier, frame_at((mine + s) % NB, core), tile)
-        return carry
-
-    lax.fori_loop(1, NB, greet, 0)
-
     has_before, has_after = tile > 0, tile < tiles - 1
     edge = ((mine < 2) & (tile == 0)) | ((mine > 5) & (tile == tiles - 1))
 
@@ -106,6 +100,12 @@
             return carry
 
         lax.fori_loop(0, NB, greet_after, 0)
+
+    def greet(s, carry):
+        signal(barrier, frame_at((mine + s) % NB, core), tile)
+        return carry
+
+    lax.fori_loop(1, NB, greet, 0)
 
     signal(barrier, sibling, tile)
 
@@ -334,13 +334,6 @@
     sibling = frame + 1 - 2 * core
 
     barrier = pltpu.get_barrier_semaphore()
-    signal(barrier, sibling, tile)
-
-    def greet(s, carry):
-        signal(barrier, frame_at((mine + s) % NB, core), tile)
-        return carry
-
-    lax.fori_loop(1, NB, greet, 0)
     has_before, has_after = tile > 0, tile < tiles - 1
 
     @pl.when(has_before)
@@ -352,6 +345,14 @@
     def _():
         for b in (0, 1):
             signal(barrier, frame_at(b, core), after)
+
+    signal(barrier, sibling, tile)
+
+    def greet(s, carry):
+        signal(barrier, frame_at((mine + s) % NB, core), tile)
+        return carry
+
+    lax.fori_loop(1, NB, greet, 0)
 
     outer = [
         (slot, first - slot + 4, last - first + 1, has_before if slot < 2 else has_after)

time: 37.1 us -> 36.8 us (level)
  Pallas kernels: 36.4 us -> 36 us
where the time goes in v6:
time: 36.8 us; the launch traced here: 36.7 us
  Pallas kernels  36 us (98%)
  between operations  0.66 us (2%)
    pallas_call x1, Pallas kernels, per_device(): pl.pallas_call(return_kernel, name='give_back', out_shape=(shape((NB, 1,...  13 us
    pallas_call x1, Pallas kernels, per_device(): pl.pallas_call(exchange_kernel, name='exchange', out_shape=(shape((ZERO +...  12.5 us
    pallas_call x1, Pallas kernels, per_device(): pl.pallas_call(compute_kernel, name='compute', out_shape=(shape((NF, 1, 1...  9.86 us

profile of v6, /device:TPU:100, one launch (start us, length us, event | category | flops | bytes accessed | tf_op | source)
XLA Modules:
  0.0 36.7 jit_solution(13762907096887780093)
XLA Ops:
  0.6 12.5 %exchange.1 = (bf16[81,32,128]{2,1,0:T(8,128)(2,1)S(1)}, s32[8,128]{1,0:T(8,128)S(1)}, f32[8,128]{1,0:T(8,128)S(1)}, bf16[16,256,256]{2,1,0:T(8,128)(2,1)S(1)}, ...) custom-call(bf16[32,1024]{1,0:T(8,128)(2,1)} %bitcast.8, s32[4,8,32]{2,1,0:T(8,128)} %bitcast.9, ...), custom_call_target="tpu_custom_call" | custom-call | tf_op jit(solution)/shard_map/exchange/pallas_call | solution.py:506
  13.1 9.9 %compute.1 = (f32[8,1,128]{2,1,0:T(1,128)S(1)}, f32[81,32,128]{2,1,0:T(8,128)S(1)}, f32[8,32,128]{2,1,0:T(8,128)S(1)}) custom-call(s32[8,128]{1,0:T(8,128)S(1)} %get-tuple-element.15.idx, bf16[81,32,128]{2,1,0:T(8,128)(2,1)S(1)} %get-tuple-element.16.win, bf16[16,256,256]{2,1,0:T(8,128)(2,1)S(1)} %get-tuple-element.17.diag, ...), custom_call_target="tpu_custom_call" | custom-call | tf_op jit(solution)/shard_map/compute/pallas_call | solution.py:539
  23.0 13.0 %give_back.1 = (f32[8,1,128]{2,1,0:T(1,128)S(1)}, bf16[12,5,32,128]{3,2,1,0:T(8,128)(2,1)S(1)}) custom-call(f32[81,32,128]{2,1,0:T(8,128)S(1)} %get-tuple-element.21.acc, f32[8,32,128]{2,1,0:T(8,128)S(1)} %get-tuple-element.22.ref_acc, f32[8,1,128]{2,1,0:T(1,128)S(1)} %get-tuple-element.23.depths), custom_call_target="tpu_custom_call" | custom-call | tf_op jit(solution)/shard_map/give_back/pallas_call | solution.py:553
  36.0 0.7 %total.1 = (f32[1,1024]{1,0:T(1,128)}, f32[32,1024]{1,0:T(8,128)}) custom-call(f32[8,1,128]{2,1,0:T(1,128)S(1)} %get-tuple-element.24.depth_rx, bf16[12,5,32,128]{3,2,1,0:T(8,128)(2,1)S(1)} %get-tuple-element.25.rx), custom_call_target="tpu_custom_call" | custom-call | tf_op jit(solution)/shard_map/total/pallas_call | solution.py:570

commit v7 on v6

--- a/solution.py
+++ b/solution.py
@@ -101,13 +101,6 @@
 
         lax.fori_loop(0, NB, greet_after, 0)
 
-    def greet(s, carry):
-        signal(barrier, frame_at((mine + s) % NB, core), tile)
-        return carry
-
-    lax.fori_loop(1, NB, greet, 0)
-
-    signal(barrier, sibling, tile)
 
     for b in range(NB):
         pltpu.make_async_copy(feats.at[:, pl.ds(b * 128, 128)], blocks.at[b], load.at[0]).start()
@@ -125,8 +118,13 @@
     ]
     for copy in small:
         copy.start()
-    for copy in half:
-        copy.start()
+    def greet(s, carry):
+        signal(barrier, frame_at((mine + s) % NB, core), tile)
+        return carry
+
+    lax.fori_loop(1, NB, greet, 0)
+
+    signal(barrier, sibling, tile)
     win[ZERO] = jnp.zeros((C, 128), bf16)
     for b, outside in ((0, (0, 1)), (1, (0,)), (6, (4,)), (7, (3, 4))):
         @pl.when((mine == b) & edge)
@@ -191,6 +189,8 @@
                 blocks.at[pl.ds(mine - 2 + at, count)], win.at[pl.ds(own * W + at, count)], recv.at[own]
             ).start()
 
+    for copy in half:
+        copy.start()
     corner = jnp.zeros((D // 2, 128, 128), bf16)
     diag[:, 0:128, 128:256] = corner
     diag[:, 128:256, 0:128] = corner

time: 36.8 us -> 36.8 us (level)
  no operation moved by 1% of the time
where the time goes in v7:
time: 36.8 us; the launch traced here: 36.7 us
  Pallas kernels  36 us (98%)
  between operations  0.66 us (2%)
    pallas_call x1, Pallas kernels, per_device(): pl.pallas_call(return_kernel, name='give_back', out_shape=(shape((NB, 1,...  13 us
    pallas_call x1, Pallas kernels, per_device(): pl.pallas_call(exchange_kernel, name='exchange', out_shape=(shape((ZERO +...  12.5 us
    pallas_call x1, Pallas kernels, per_device(): pl.pallas_call(compute_kernel, name='compute', out_shape=(shape((NF, 1, 1...  9.86 us

profile of v7, /device:TPU:100, one launch (start us, length us, event | category | flops | bytes accessed | tf_op | source)
XLA Modules:
  0.0 36.7 jit_solution(5335009077545044525)
XLA Ops:
  0.6 12.5 %exchange.1 = (bf16[81,32,128]{2,1,0:T(8,128)(2,1)S(1)}, s32[8,128]{1,0:T(8,128)S(1)}, f32[8,128]{1,0:T(8,128)S(1)}, bf16[16,256,256]{2,1,0:T(8,128)(2,1)S(1)}, ...) custom-call(bf16[32,1024]{1,0:T(8,128)(2,1)} %bitcast.8, s32[4,8,32]{2,1,0:T(8,128)} %bitcast.9, ...), custom_call_target="tpu_custom_call" | custom-call | tf_op jit(solution)/shard_map/exchange/pallas_call | solution.py:506
  13.1 9.9 %compute.1 = (f32[8,1,128]{2,1,0:T(1,128)S(1)}, f32[81,32,128]{2,1,0:T(8,128)S(1)}, f32[8,32,128]{2,1,0:T(8,128)S(1)}) custom-call(s32[8,128]{1,0:T(8,128)S(1)} %get-tuple-element.15.idx, bf16[81,32,128]{2,1,0:T(8,128)(2,1)S(1)} %get-tuple-element.16.win, bf16[16,256,256]{2,1,0:T(8,128)(2,1)S(1)} %get-tuple-element.17.diag, ...), custom_call_target="tpu_custom_call" | custom-call | tf_op jit(solution)/shard_map/compute/pallas_call | solution.py:539
  23.0 13.0 %give_back.1 = (f32[8,1,128]{2,1,0:T(1,128)S(1)}, bf16[12,5,32,128]{3,2,1,0:T(8,128)(2,1)S(1)}) custom-call(f32[81,32,128]{2,1,0:T(8,128)S(1)} %get-tuple-element.21.acc, f32[8,32,128]{2,1,0:T(8,128)S(1)} %get-tuple-element.22.ref_acc, f32[8,1,128]{2,1,0:T(1,128)S(1)} %get-tuple-element.23.depths), custom_call_target="tpu_custom_call" | custom-call | tf_op jit(solution)/shard_map/give_back/pallas_call | solution.py:553
  36.0 0.7 %total.1 = (f32[1,1024]{1,0:T(1,128)}, f32[32,1024]{1,0:T(8,128)}) custom-call(f32[8,1,128]{2,1,0:T(1,128)S(1)} %get-tuple-element.24.depth_rx, bf16[12,5,32,128]{3,2,1,0:T(8,128)(2,1)S(1)} %get-tuple-element.25.rx), custom_call_target="tpu_custom_call" | custom-call | tf_op jit(solution)/shard_map/total/pallas_call | solution.py:570
